TPU v7x, 32 devices: a whole 2x2x4 slice. The times are simulated.
32 devices in a mesh: scan: 4 (over y, x), blk: 8 (over z, core).
Axes of the slice: x: 2, y: 2, z: 4, core: 2. Of those that a mesh axis runs over, the one named last changes fastest.
Arguments:
- ref_feats: bfloat16 [4, 4096, 256], P('scan', 'blk'), may hold values from -120 to 120
- src_feats: bfloat16 [4, 1024, 256], P('scan', 'blk'), may hold values from -120 to 120
- grad_out: bfloat16 [4, 4096, 256], P('scan', 'blk'), may hold values from -6 to 6
- w_query: bfloat16 [256, 256], replicated, may hold values from -1 to 1
- w_key: bfloat16 [256, 256], replicated, may hold values from -1 to 1
- w_value: bfloat16 [256, 256], replicated, may hold values from -0.375 to 0.375
- w_out: bfloat16 [256, 256], replicated, may hold values from -0.375 to 0.375
- intersection: int32 [4, 32, 8], P('scan', 'blk'), may hold values from 0 to 1, as said below
Outputs:
- matched: bfloat16 [4, 4096, 256], P('scan', 'blk')
- grad_ref: bfloat16 [4, 4096, 256], P('scan', 'blk')
- grad_src: bfloat16 [4, 1024, 256], P('scan', 'blk')
- grad_w_query: float32 [256, 256], replicated
- grad_w_key: float32 [256, 256], replicated
- grad_w_value: float32 [256, 256], replicated
- grad_w_out: float32 [256, 256], replicated
Inputs may be any that keep to these rules, and one draw needn't show every extreme that they name: intersection[p, b, c] is 1 for c = b * 8 // 32, so every reference block and every source block of a pair has a listed partner.
All inputs are finite; a program needn't handle non-finite values.
Results may differ from a plain program's by a relative error of at most 0.035.
Values may be sent and summed in bfloat16 or wider, within the bound.
No kernel may reach another device: no remote copies, remote signals or barrier semaphores. Data moves between devices by JAX's collectives and lax.ppermute only.
A program may use at most 64 MiB of HBM per device.

v0:
```python
import functools
import math

import jax
import jax.numpy as jnp
from jax import lax
from jax.experimental import pallas as pl
from jax.experimental.pallas import tpu as pltpu
from jax.sharding import PartitionSpec as P

HEADS = 4
BLOCK = 128
NEG = -1e30
FLOOR = -1e29
LOG2E = math.log2(math.e)

NT = (((1,), (1,)), ((), ()))
TN = (((0,), (0,)), ((), ()))
TT = (((0,), (1,)), ((), ()))


def mm(left, right):
    return jnp.dot(left, right, preferred_element_type=jnp.float32)


def mm_general(left, right, dims):
    return lax.dot_general(left, right, dims, preferred_element_type=jnp.float32)


def bf(x):
    return x.astype(jnp.bfloat16)


def lane_row(width, head, head_dim):
    lanes = lax.broadcasted_iota(jnp.int32, (1, width), 1) // head_dim
    return bf(jnp.where(lanes == head, 1.0, 0.0))


def spread(reduced, like):
    return jnp.broadcast_to(reduced, like.shape)


STRIP = 32
STEP = 256


def by_eight(x):
    return x.reshape(x.shape[0] // 8, 8, x.shape[1])


def listed_steps(inter_ref, query_block, work):
    per_step = STEP // BLOCK

    def visit(step, carry):
        listed = [inter_ref[query_block, step * per_step + k] == 1 for k in range(per_step)]

        @pl.when(functools.reduce(jnp.logical_or, listed))
        def _():
            work(query_block, step, listed)

        return carry

    lax.fori_loop(0, inter_ref.shape[1] // per_step, visit, 0)


def each_listed(inter_ref, work):
    def visit(query_block, carry):
        listed_steps(inter_ref, query_block, work)
        return carry

    lax.fori_loop(0, inter_ref.shape[0], visit, 0)


def head_strips(heads):
    for head in range(heads):
        spans = [slice(first, first + STRIP) for first in range(0, BLOCK, STRIP)]
        yield head, [slice(head * BLOCK + a.start, head * BLOCK + a.stop) for a in spans]


def score_block(query_block, step, listed, left_ref, key_t_ref, score_ref):
    span = pl.ds(pl.multiple_of(step * STEP, STEP), STEP)
    bias = jnp.concatenate(
        [jnp.full((1, BLOCK), jnp.where(flag, 0.0, NEG), jnp.float32) for flag in listed], axis=1
    )
    score_ref[...] = mm(left_ref[query_block], key_t_ref[:, span]) * LOG2E + bias


def unpack(packed_ref, count):
    total, width = packed_ref.shape
    rows = (total - 2 * width) // 2
    sizes = [rows] * (count - 2) + [width, width]
    return [packed_ref.at[pl.ds(sum(sizes[:k]), sizes[k])] for k in range(count)]


def project_kernel(heads, near_ref, left_ref, gleft_ref):
    ref_ref, gout_ref, wq_ref, wo_ref = unpack(near_ref, 4)
    rows, width = ref_ref.shape
    head_dim = width // heads
    query = bf(bf(mm(ref_ref[...], wq_ref[...])).astype(jnp.float32) * head_dim ** -0.5)
    grad = bf(mm_general(gout_ref[...], wo_ref[...], NT))
    for query_block in range(rows // BLOCK):
        span = slice(query_block * BLOCK, (query_block + 1) * BLOCK)
        for head in range(heads):
            own = lane_row(width, head, head_dim)
            left_ref[query_block, head * BLOCK : (head + 1) * BLOCK, :] = query[span] * own
            gleft_ref[query_block, head * BLOCK : (head + 1) * BLOCK, :] = grad[span] * own


def stats_kernel(
    heads, inter_ref, left_ref, gleft_ref, far_ref, src_ref,
    peak_ref, inverse_ref, col_ref, score_ref, product_ref,
    key_t_ref, value_t_ref, prob_ref, total_ref, col_peak_ref, col_total_ref, col_dot_ref,
):
    wk_ref, wv_ref = unpack(far_ref, 2)
    rows, key_total = left_ref.shape[0] * BLOCK, src_ref.shape[0]
    key_t_ref[...] = bf(mm_general(wk_ref[...], src_ref[...], TT))
    value_t_ref[...] = bf(mm_general(wv_ref[...], src_ref[...], TT))
    steps = key_total // STEP
    peak_ref[...] = jnp.full(peak_ref.shape, 2.0 * NEG, jnp.float32)
    total_ref[...] = jnp.zeros(total_ref.shape, jnp.float32)
    col_peak_ref[...] = jnp.full(col_peak_ref.shape, FLOOR, jnp.float32)
    col_total_ref[...] = jnp.zeros(col_total_ref.shape, jnp.float32)
    col_dot_ref[...] = jnp.zeros(col_dot_ref.shape, jnp.float32)
    tiles = [slice(first, first + 128) for first in range(0, STEP, 128)]

    def peaks(query_block, step, listed):
        block_ref = score_ref.at[query_block * steps + step]
        score_block(query_block, step, listed, left_ref, key_t_ref, block_ref)
        for head, spans in head_strips(heads):
            col_peaks = [col_peak_ref[step, head, :, lanes] for lanes in tiles]
            for span in spans:
                row_peak = peak_ref[query_block, span, :]
                for at, lanes in enumerate(tiles):
                    scores = block_ref[span, lanes]
                    row_peak = jnp.maximum(row_peak, scores)
                    col_peaks[at] = jnp.maximum(col_peaks[at], by_eight(scores).max(axis=0))
                peak_ref[query_block, span, :] = row_peak
            for at, lanes in enumerate(tiles):
                col_peak_ref[step, head, :, lanes] = col_peaks[at]

    each_listed(inter_ref, peaks)
    for query_block in range(rows // BLOCK):
        peak = peak_ref[query_block]
        peak_ref[query_block] = spread(peak.max(axis=1, keepdims=True), peak)
    for step in range(steps):
        for head in range(heads):
            peak = col_peak_ref[step, head]
            col_peak_ref[step, head] = spread(peak.max(axis=0, keepdims=True), peak)

    def totals(query_block, step, listed):
        score_now, product_now = [
            ref.at[query_block * steps + step] for ref in (score_ref, product_ref)
        ]
        span = pl.ds(pl.multiple_of(step * STEP, STEP), STEP)
        prob_ref[...] = mm(gleft_ref[query_block], value_t_ref[:, span])
        for head, spans in head_strips(heads):
            col_totals = [col_total_ref[step, head, :, lanes] for lanes in tiles]
            for span in spans:
                row_peak = by_eight(peak_ref[query_block, span, :])
                row_total = by_eight(total_ref[query_block, span, :])
                for at, lanes in enumerate(tiles):
                    scores = by_eight(score_now[span, lanes])
                    row_exp = jnp.exp2(scores - row_peak)
                    col_exp = jnp.exp2(scores - col_peak_ref[step, head, :, lanes][None])
                    row_total = row_total + row_exp
                    product = row_exp * col_exp * by_eight(prob_ref[span, lanes])
                    product_now[span, lanes] = bf(product.reshape(STRIP, 128))
                    col_totals[at] = col_totals[at] + col_exp.sum(axis=0)
                total_ref[query_block, span, :] = row_total.reshape(STRIP, 128)
            for at, lanes in enumerate(tiles):
                col_total_ref[step, head, :, lanes] = col_totals[at]

    each_listed(inter_ref, totals)
    for query_block in range(rows // BLOCK):
        total = total_ref[query_block]
        inverse_ref[query_block] = spread(1.0 / total.sum(axis=1, keepdims=True), total)

    def dots(query_block, step, listed):
        product_now = product_ref.at[query_block * steps + step]
        for head, spans in head_strips(heads):
            col_dots = [col_dot_ref[step, head, :, lanes] for lanes in tiles]
            for span in spans:
                inverse = inverse_ref[query_block, span, :]
                for at, lanes in enumerate(tiles):
                    product = by_eight(product_now[span, lanes].astype(jnp.float32) * inverse)
                    col_dots[at] = col_dots[at] + product.sum(axis=0)
            for at, lanes in enumerate(tiles):
                col_dot_ref[step, head, :, lanes] = col_dots[at]

    each_listed(inter_ref, dots)
    for step in range(steps):
        lanes = slice(step * STEP, (step + 1) * STEP)
        for head in range(heads):
            mine = slice(head, head + 1)
            col_ref[0, mine, lanes] = col_peak_ref[step, head, 0:1, :]
            col_ref[1, mine, lanes] = col_total_ref[step, head].sum(axis=0, keepdims=True)
            col_ref[2, mine, lanes] = col_dot_ref[step, head].sum(axis=0, keepdims=True)


def side_kernel(
    heads, near_ref, far_ref, src_ref, key_ref, value_ref, query_t_ref, grad_t_ref
):
    ref_ref, gout_ref, wq_ref, wo_ref = unpack(near_ref, 4)
    wk_ref, wv_ref = unpack(far_ref, 2)
    rows, width = ref_ref.shape
    head_dim = width // heads
    key_ref[...] = bf(mm(src_ref[...], wk_ref[...]))
    value_ref[...] = bf(mm(src_ref[...], wv_ref[...]))
    query_t = bf(mm_general(wq_ref[...], ref_ref[...], TT)).astype(jnp.float32)
    query_t = bf(query_t * (2.0 * head_dim ** -0.5))
    grad_t = bf(mm_general(wo_ref[...], gout_ref[...], NT))
    for values, out_ref in ((query_t, query_t_ref), (grad_t, grad_t_ref)):
        out_ref[...] = jnp.zeros(out_ref.shape, jnp.bfloat16)
        for query_block in range(rows // BLOCK):
            span = slice(query_block * BLOCK, (query_block + 1) * BLOCK)
            for head in range(heads):
                mine = slice(head * head_dim, (head + 1) * head_dim)
                lanes = slice(head * BLOCK, (head + 1) * BLOCK)
                out_ref[query_block, mine, lanes] = values[mine, span]


def grads_kernel(
    heads, inter_ref, score_ref, product_ref, key_ref, value_ref,
    query_t_ref, grad_t_ref, peak_ref, inverse_ref, own_ref, near_ref, far_ref, packed_ref, src_ref,
    attended_ref, gquery_ref, gkey_ref, gvalue_ref, weight_ref,
    rest_ref, match_ref, gscore_ref, dot_ref, col_ref,
    att_ref, gq_ref, gk_ref, gv_ref,
):
    ref_ref, gout_ref = unpack(packed_ref, 4)[:2]
    rows, width = ref_ref.shape
    key_total = src_ref.shape[0]
    steps = key_total // STEP
    head_dim = width // heads
    tiles = [slice(first, first + 128) for first in range(0, STEP, 128)]

    peak = jnp.maximum(near_ref[0], far_ref[0])
    near, far = jnp.exp2(near_ref[0] - peak), jnp.exp2(far_ref[0] - peak)
    inverse = 1.0 / (near * near_ref[1] + far * far_ref[1])
    half = (near * near_ref[2] + far * far_ref[2]) * inverse * 0.5
    factor = jnp.exp2(own_ref[0] - peak) * inverse
    for kind, values in enumerate((peak, inverse, factor, half)):
        for head in range(heads):
            for step in range(steps):
                piece = values[head : head + 1, step * STEP : (step + 1) * STEP]
                col_ref[kind, step, head] = jnp.broadcast_to(piece, (8, STEP))
    for ref in (att_ref, gq_ref, gk_ref, gv_ref):
        ref[...] = jnp.zeros(ref.shape, jnp.float32)

    def products(query_block, step, listed):
        score_now, product_now = [
            ref.at[query_block * steps + step] for ref in (score_ref, product_ref)
        ]
        rest_now, match_now = rest_ref.at[step], match_ref.at[step]
        for head, spans in head_strips(heads):
            for span in spans:
                row_peak = by_eight(peak_ref[query_block, span, :])
                row_inverse = by_eight(inverse_ref[query_block, span, :])
                row_dot = by_eight(dot_ref[span, :])
                for lanes in tiles:
                    col_peak, col_inverse, col_factor, col_half = [
                        col_ref[kind, step, head, :, lanes][None] for kind in range(4)
                    ]
                    scores = by_eight(score_now[span, lanes])
                    row_prob = jnp.exp2(scores - row_peak) * row_inverse
                    col_prob = jnp.exp2(scores - col_peak) * col_inverse
                    product = by_eight(product_now[span, lanes].astype(jnp.float32))
                    product = product * row_inverse * col_factor
                    row_dot = row_dot + product
                    match_now[span, lanes] = bf((row_prob * col_prob).reshape(STRIP, 128))
                    rest_now[span, lanes] = (product - col_prob * col_half).reshape(STRIP, 128)
                dot_ref[span, :] = row_dot.reshape(STRIP, 128)

    def own_lanes(stacked):
        total = None
        for head in range(heads):
            own = lane_row(width, head, head_dim).astype(jnp.float32)
            piece = stacked[head * BLOCK : (head + 1) * BLOCK] * own
            total = piece if total is None else total + piece
        return total

    def outputs(query_block, step, listed):
        score_now, rest_now, match_now = [
            score_ref.at[query_block * steps + step], rest_ref.at[step], match_ref.at[step]
        ]
        for _, spans in head_strips(heads):
            for span in spans:
                row_peak = peak_ref[query_block, span, :]
                row_half = dot_ref[span, :] * inverse_ref[query_block, span, :]
                for lanes in tiles:
                    row_part = jnp.exp2(score_now[span, lanes] - row_peak) * row_half
                    gscore_ref[span, lanes] = bf(rest_now[span, lanes] - row_part)
        span = pl.ds(pl.multiple_of(step * STEP, STEP), STEP)
        att_ref[query_block] += own_lanes(mm(match_now[...], value_ref[span, :]))
        gq_ref[query_block] += own_lanes(mm(gscore_ref[...], key_ref[span, :]))
        gk_ref[step] += mm(query_t_ref[query_block], gscore_ref[...])
        gv_ref[step] += mm(grad_t_ref[query_block], match_now[...])

    def query_rows(query_block, carry):
        dot_ref[...] = jnp.zeros(dot_ref.shape, jnp.float32)
        listed_steps(inter_ref, query_block, products)
        dot = dot_ref[...]
        dot_ref[...] = spread(dot.sum(axis=1, keepdims=True) * 0.5, dot)
        listed_steps(inter_ref, query_block, outputs)
        return carry

    lax.fori_loop(0, rows // BLOCK, query_rows, 0)
    attended = bf(att_ref[...]).reshape(rows, width)
    gquery = bf(gq_ref[...] * (2.0 * head_dim ** -0.5)).reshape(rows, width)
    attended_ref[...] = attended
    gquery_ref[...] = gquery
    for step in range(steps):
        gkey_ref[:, step * STEP : (step + 1) * STEP] = bf(gk_ref[step])
        gvalue_ref[:, step * STEP : (step + 1) * STEP] = bf(gv_ref[step])
    weight_ref[0] = bf(mm_general(ref_ref[...], gquery, TN))
    weight_ref[1] = bf(mm(gkey_ref[...], src_ref[...]).T)
    weight_ref[2] = bf(mm(gvalue_ref[...], src_ref[...]).T)
    weight_ref[3] = bf(mm_general(attended, gout_ref[...], TN))


def source_kernel(far_ref, gkey_ref, gvalue_ref, gsrc_ref):
    wk_ref, wv_ref = unpack(far_ref, 2)
    gsrc_t = mm(wk_ref[...], gkey_ref[...]) + mm(wv_ref[...], gvalue_ref[...])
    gsrc_ref[...] = bf(gsrc_t.T)


def rows_kernel(near_ref, attended_ref, gquery_ref, matched_ref, gref_ref):
    ref_ref, gout_ref, wq_ref, wo_ref = unpack(near_ref, 4)
    matched = ref_ref[...].astype(jnp.float32) + mm(attended_ref[...], wo_ref[...])
    matched_ref[...] = bf(matched)
    gref = gout_ref[...].astype(jnp.float32) + mm_general(gquery_ref[...], wq_ref[...], NT)
    gref_ref[...] = bf(gref)


def swap(x, axis, apart):
    pairs = [(i, i ^ apart) for i in range(lax.axis_size(axis))]
    return lax.ppermute(x, axis, pairs)


def at(x, index, axis=0):
    return lax.dynamic_index_in_dim(x, index, axis, False)


def laid(near, far, side, axis=0):
    shape = near.shape[:axis] + (2,) + near.shape[axis:]
    out = lax.dynamic_update_index_in_dim(jnp.zeros(shape, near.dtype), near, side, axis)
    return lax.dynamic_update_index_in_dim(out, far, 1 - side, axis)


def add(near, far):
    return (near.astype(jnp.float32) + far.astype(jnp.float32)).astype(near.dtype)


def halve(x, step, axis=0):
    mesh_axis, bit, side = step
    return add(at(x, side, axis), swap(at(x, 1 - side, axis), mesh_axis, bit))


def double(x, step, axis=0):
    mesh_axis, bit, side = step
    return laid(x, swap(x, mesh_axis, bit), side, axis)


def bit_steps(mesh_axis):
    me = lax.axis_index(mesh_axis)
    bits = range(lax.axis_size(mesh_axis).bit_length() - 1)
    return [(mesh_axis, 1 << bit, (me >> bit) % 2) for bit in bits]


def scatter_direct(x, mesh_axis):
    me, count = lax.axis_index(mesh_axis), lax.axis_size(mesh_axis)
    total = at(x, me).astype(jnp.float32)
    for piece in [swap(at(x, me ^ apart), mesh_axis, apart) for apart in range(1, count)]:
        total = total + piece.astype(jnp.float32)
    return total.astype(x.dtype)


def gather_direct(x, mesh_axis):
    me, count = lax.axis_index(mesh_axis), lax.axis_size(mesh_axis)
    pieces = [x] + [swap(x, mesh_axis, apart) for apart in range(1, count)]
    out = jnp.zeros((count,) + x.shape, x.dtype)
    for apart, piece in enumerate(pieces):
        out = lax.dynamic_update_index_in_dim(out, piece, me ^ apart, 0)
    return out


def combine_stats(parts):
    peak = functools.reduce(jnp.maximum, [part[0] for part in parts])
    factors = [jnp.exp2(part[0] - peak) for part in parts]
    total = sum(factor * part[1] for factor, part in zip(factors, parts))
    dots = sum(factor * part[2] for factor, part in zip(factors, parts))
    return jnp.stack([peak, total, dots])


def vmem_call(kernel, name, out_shape, scratch, limit, flops, moved, args, scalars=0):
    specs = [pl.BlockSpec(memory_space=pltpu.SMEM)] * scalars
    specs += [pl.BlockSpec(memory_space=pltpu.VMEM)] * (len(args) - scalars)
    return pl.pallas_call(
        kernel,
        name=name,
        out_shape=out_shape,
        in_specs=specs,
        out_specs=[pl.BlockSpec(memory_space=pltpu.VMEM)] * len(out_shape),
        scratch_shapes=scratch,
        compiler_params=pltpu.CompilerParams(vmem_limit_bytes=limit),
        cost_estimate=pl.CostEstimate(flops=flops, bytes_accessed=moved, transcendentals=0),
    )(*args)


def on_device(ref_feats, src_feats, grad_out, w_query, w_key, w_value, w_out, intersection):
    ref_rows = ref_feats[0]
    src_rows = src_feats[0]
    out_grad = grad_out[0]
    listed = jnp.where(intersection[0] == 1, 1, 0)
    rows, width = ref_rows.shape
    core_step = bit_steps("core")[0]
    chip_steps = bit_steps("chip")
    key_rows = src_rows.shape[0]
    key_total = key_rows * lax.axis_size("chip") * lax.axis_size("core")

    source_all = src_rows
    projections = (w_query, w_out, w_key, w_value)
    for count, step in enumerate(chip_steps[::-1]):
        source_all = double(source_all, step, count)
        if count == 0:
            source_all, projections = lax.optimization_barrier((source_all, projections))
    near_pack = jnp.concatenate([ref_rows, out_grad, *projections[:2]], axis=0)
    far_pack = jnp.concatenate(projections[2:], axis=0)
    source_all = double(source_all, core_step, len(chip_steps)).reshape(key_total, width)

    f32, b16 = jnp.float32, jnp.bfloat16
    shape, vmem = jax.ShapeDtypeStruct, pltpu.VMEM
    unit = 2 * rows * width * width
    query_blocks, steps = rows // BLOCK, key_total // STEP
    stacked = HEADS * BLOCK
    blocks = (query_blocks * steps, stacked, STEP)
    row_like = (query_blocks, stacked, 128)
    col_like = vmem((steps, HEADS, 8, STEP), f32)
    room = (16 << 20) + max(0, rows * key_total * HEADS * 18 - (36 << 20))
    left, grad_left = vmem_call(
        functools.partial(project_kernel, HEADS),
        "project_reference",
        [
            shape((query_blocks, stacked, width), b16),
            shape((query_blocks, stacked, width), b16),
        ],
        [],
        8 << 20,
        4 * unit,
        1 << 20,
        (near_pack,),
    )
    row_peak, row_inverse, col_stats, scores, product = vmem_call(
        functools.partial(stats_kernel, HEADS),
        "match_stats",
        [
            shape(row_like, f32),
            shape(row_like, f32),
            shape((3, HEADS, key_total), f32),
            shape(blocks, f32),
            shape(blocks, b16),
        ],
        [
            vmem((width, key_total), b16),
            vmem((width, key_total), b16),
            vmem((stacked, STEP), f32),
            vmem(row_like, f32),
            col_like,
            col_like,
            col_like,
        ],
        room,
        60 * unit,
        8 << 20,
        (listed, left, grad_left, far_pack, source_all),
        scalars=1,
    )
    near_stats = col_stats
    keys, values, query_t, grad_t = vmem_call(
        functools.partial(side_kernel, HEADS),
        "project_for_grads",
        [
            shape((key_total, width), b16),
            shape((key_total, width), b16),
            shape((query_blocks, width, stacked), b16),
            shape((query_blocks, width, stacked), b16),
        ],
        [],
        8 << 20,
        8 * unit,
        2 << 20,
        (near_pack, far_pack, source_all),
    )
    for mesh_axis, bit, _ in chip_steps:
        near_stats = combine_stats([near_stats, swap(near_stats, mesh_axis, bit)])
    far_stats = swap(near_stats, "core", 1)
    attended, grad_query, grad_key, grad_value, weight_part = vmem_call(
        functools.partial(grads_kernel, HEADS),
        "match_grads",
        [
            shape((rows, width), b16),
            shape((rows, width), b16),
            shape((width, key_total), b16),
            shape((width, key_total), b16),
            shape((4, width, width), b16),
        ],
        [
            vmem((steps, stacked, STEP), f32),
            vmem((steps, stacked, STEP), b16),
            vmem((stacked, STEP), b16),
            vmem((stacked, 128), f32),
            vmem((4, steps, HEADS, 8, STEP), f32),
            vmem((query_blocks, BLOCK, width), f32),
            vmem((query_blocks, BLOCK, width), f32),
            vmem((steps, width, STEP), f32),
            vmem((steps, width, STEP), f32),
        ],
        room,
        100 * unit,
        8 << 20,
        (listed, scores, product, keys, values, query_t, grad_t, row_peak, row_inverse, col_stats,
         near_stats, far_stats, near_pack, source_all),
        scalars=1,
    )
    (source_part,) = vmem_call(
        source_kernel,
        "source_grads",
        [shape((key_total, width), b16)],
        [],
        8 << 20,
        8 * unit,
        2 << 20,
        (far_pack, grad_key, grad_value),
    )

    scans = lax.axis_size("scan")
    weights = weight_part.reshape((2, scans // 2, 2, -1, width))
    sources = source_part.reshape((2,) * (len(chip_steps) + 1) + (key_rows, width))
    source_steps = chip_steps[::-1]
    weights = halve(weights, core_step)
    sources = halve(sources, core_step, len(chip_steps))
    weights, sources = lax.optimization_barrier((weights, sources))
    weights = scatter_direct(weights.reshape((scans,) + weights.shape[2:]), "scan")
    sources = halve(sources, source_steps[0])
    weights, sources, attended, grad_query = lax.optimization_barrier(
        (weights, sources, attended, grad_query)
    )
    matched, grad_ref = vmem_call(
        rows_kernel,
        "row_outputs",
        [shape((rows, width), b16), shape((rows, width), b16)],
        [],
        8 << 20,
        4 * unit,
        2 << 20,
        (near_pack, attended, grad_query),
    )
    for step in source_steps[1:]:
        sources = halve(sources, step)
    for mesh_axis, bit, _ in chip_steps:
        weights = add(weights, swap(weights, mesh_axis, bit))
    weights, grad_src = lax.optimization_barrier((weights, sources))
    weights = gather_direct(weights, "scan")
    weights = double(weights, core_step)
    weights = weights.reshape(4, width, width).astype(f32)
    return (
        matched[None],
        grad_ref[None],
        grad_src[None],
        weights[0],
        weights[1],
        weights[2],
        weights[3],
    )


def solution(mesh):
    scans, blks = mesh.shape["scan"], mesh.shape["blk"]
    mesh = jax.sharding.Mesh(
        mesh.devices.reshape(scans, blks // 2, 2), ("scan", "chip", "core")
    )
    split = P("scan", ("chip", "core"), None)
    whole = P()
    return jax.shard_map(
        on_device,
        mesh=mesh,
        in_specs=(split, split, split, whole, whole, whole, whole, split),
        out_specs=(split, split, split, whole, whole, whole, whole),
        check_vma=False,
    )
```

profile of v0, /device:TPU:0, one launch (start us, length us, event | category | flops | bytes accessed | tf_op | source)
XLA Modules:
  0.0 82.4 jit_solution(3590487679454523244)
XLA Ops:
  0.7 4.1 %collective-permute-start = (bf16[128,256]{1,0:T(8,128)(2,1)}, bf16[128,256]{1,0:T(8,128)(2,1)S(1)}, u32[]{:S(2)}, u32[]{:S(2)}) collective-permute-start(bf16[128,256]{1,0:T(8,128)(2,1)} %bitcast.92), channel_id=1, source_target_pairs={{0,4},{2,6},{4,0},{6,2},{1,5},{3,7},{5,1},{7,3},{8,12},{10,14},{12... | collective-permute-start | bytes 196616 | tf_op jit(solution)/shard_map/ppermute | solution.py:336
  5.5 0.9 %constant_dynamic-update-slice_fusion.2 = bf16[2,128,256]{2,1,0:T(8,128)(2,1)S(1)} fusion(bf16[2,128,256]{2,1,0:T(8,128)(2,1)S(1)} %broadcast_in_dim.69, bf16[1,128,256]{2,1,0:T(8,128)(2,1)} %param.9, s32[]{:T(128)S(6)} %select_n.76), kind=kLoop, calls=%fused_computation.55 | loop fusion | bytes 131076 | tf_op jit(solution)/shard_map/jit(dynamic_update_index_in_dim)/dynamic_update_slice | solution.py:345
  6.3 2.3 %collective-permute-done = bf16[128,256]{1,0:T(8,128)(2,1)S(1)} collective-permute-done((bf16[128,256]{1,0:T(8,128)(2,1)}, bf16[128,256]{1,0:T(8,128)(2,1)S(1)}, u32[]{:S(2)}, u32[]{:S(2)}) %collective-permute-start) | collective-permute-done | bytes 65568 | tf_op jit(solution)/shard_map/ppermute | solution.py:336
  9.4 1.2 %pad_maximum_fusion.near_ref.packed_ref = bf16[1536,256]{1,0:T(8,128)(2,1)S(1)} fusion(bf16[256,256]{1,0:T(8,128)(2,1)} %param.14, bf16[256,256]{1,0:T(8,128)(2,1)} %param.11, bf16[512,256]{1,0:T(8,128)(2,1)} %bitcast.89, bf16[512,256]{1,0:T(8,128)(2,1)} %bitcast.90), kind=kLoop, calls=%fused_computation | loop fusion | flops 3145728 | bytes 1572864 | tf_op jit(solution)/shard_map/concatenate | solution.py:426
  10.7 3.0 %collective-permute-done.1 = bf16[2,128,256]{2,1,0:T(8,128)(2,1)S(1)} collective-permute-done((bf16[2,128,256]{2,1,0:T(8,128)(2,1)S(1)}, bf16[2,128,256]{2,1,0:T(8,128)(2,1)S(1)}, u32[]{:S(2)}, u32[]{:S(2)}) %collective-permute-start.1) | collective-permute-done | bytes 131104 | tf_op jit(solution)/shard_map/ppermute | solution.py:336
  14.2 1.1 %collective-permute-done.2 = bf16[2,2,128,256]{3,2,1,0:T(8,128)(2,1)S(1)} collective-permute-done((bf16[2,2,128,256]{3,2,1,0:T(8,128)(2,1)S(1)}, bf16[2,2,128,256]{3,2,1,0:T(8,128)(2,1)S(1)}, u32[]{:S(2)}, u32[]{:S(2)}) %collective-permute-start.2) | collective-permute-done | bytes 262176 | tf_op jit(solution)/shard_map/ppermute | solution.py:336
  15.3 9.2 %match_stats.1 = (f32[4,512,128]{2,1,0:T(8,128)S(1)}, f32[4,512,128]{2,1,0:T(8,128)S(1)}, f32[3,4,1024]{2,1,0:T(4,128)S(1)}, f32[16,512,256]{2,1,0:T(8,128)S(1)}, bf16[16,512,256]{2,1,0:T(8,128)(2,1)S(1)}) custom-call(s32[4,8]{1,0:T(4,128)S(1)} %select_bitcast_fusion.inter_ref, bf16[4,512,256]{2,1,0:T(8,128)(2,1)S(1)} %get-tuple-element.40.left_ref, ...), custom_call_target="tpu_custom_call" | custom-call | flops 4026531840 | bytes 8388608 | tf_op jit(solution)/shard_map/match_stats/pallas_call | solution.py:397
  24.6 4.1 %collective-permute-done.3 = f32[3,4,1024]{2,1,0:T(4,128)S(1)} collective-permute-done((f32[3,4,1024]{2,1,0:T(4,128)S(1)}, f32[3,4,1024]{2,1,0:T(4,128)S(1)}, u32[]{:S(2)}, u32[]{:S(2)}) %collective-permute-start.3) | collective-permute-done | bytes 49184 | tf_op jit(solution)/shard_map/ppermute | solution.py:336
  28.7 2.7 %collective-permute-start.4 = (f32[3,4,1024]{2,1,0:T(4,128)S(1)}, f32[3,4,1024]{2,1,0:T(4,128)S(1)}, u32[]{:S(2)}, u32[]{:S(2)}) collective-permute-start(f32[3,4,1024]{2,1,0:T(4,128)S(1)} %pad_maximum_fusion.1), channel_id=1, source_target_pairs={{0,4},{2,6},{4,0},{6,2},{1,5},{3,7},{5,1},{7,3},{8,12},{10,14},{12... | collective-permute-start | bytes 147464 | tf_op jit(solution)/shard_map/ppermute | solution.py:336
  31.4 2.4 %collective-permute-done.4 = f32[3,4,1024]{2,1,0:T(4,128)S(1)} collective-permute-done((f32[3,4,1024]{2,1,0:T(4,128)S(1)}, f32[3,4,1024]{2,1,0:T(4,128)S(1)}, u32[]{:S(2)}, u32[]{:S(2)}) %collective-permute-start.4) | collective-permute-done | bytes 49184 | tf_op jit(solution)/shard_map/ppermute | solution.py:336
  35.1 11.0 %match_grads.1 = (bf16[512,256]{1,0:T(8,128)(2,1)S(1)}, bf16[512,256]{1,0:T(8,128)(2,1)S(1)}, bf16[256,1024]{1,0:T(8,128)(2,1)S(1)}, bf16[256,1024]{1,0:T(8,128)(2,1)S(1)}, bf16[4,256,256]{2,1,0:T(8,128)(2,1)S(1)}) custom-call(s32[4,8]{1,0:T(4,128)S(1)} %select_bitcast_fusion.inter_ref, f32[16,512,256]{2,1,0:T(8,128)S(1)} %get-tuple-element.45.score_ref, ...), custom_call_target="tpu_custom_call" | custom-call | flops 6710886400 | bytes 8388608 | tf_op jit(solution)/shard_map/match_grads/pallas_call | solution.py:397
  47.4 0.9 %collective-permute-done.7 = bf16[2,2,128,256]{3,2,1,0:T(8,128)(2,1)S(1)} collective-permute-done((bf16[2,2,128,256]{3,2,1,0:T(8,128)(2,1)S(1)}, bf16[2,2,128,256]{3,2,1,0:T(8,128)(2,1)S(1)}, u32[]{:S(2)}, u32[]{:S(2)}) %collective-permute-start.7) | collective-permute-done | bytes 262176 | tf_op jit(solution)/shard_map/ppermute | solution.py:336
  48.8 4.6 %collective-permute-start.10 = (bf16[128,256]{1,0:T(8,128)(2,1)S(1)}, bf16[128,256]{1,0:T(8,128)(2,1)S(1)}, u32[]{:S(2)}, u32[]{:S(2)}) collective-permute-start(bf16[128,256]{1,0:T(8,128)(2,1)S(1)} %get-tuple-element.76), channel_id=1, source_target_pairs={{0,24},{8,16},{16,8},{24,0},{1,25},{9,17},{17,9},{25,1},{2,26},{10... | collective-permute-start | bytes 196616 | tf_op jit(solution)/shard_map/ppermute | solution.py:336
  54.1 2.1 %collective-permute-done.10 = bf16[128,256]{1,0:T(8,128)(2,1)S(1)} collective-permute-done((bf16[128,256]{1,0:T(8,128)(2,1)S(1)}, bf16[128,256]{1,0:T(8,128)(2,1)S(1)}, u32[]{:S(2)}, u32[]{:S(2)}) %collective-permute-start.10) | collective-permute-done | bytes 65568 | tf_op jit(solution)/shard_map/ppermute | solution.py:336
  56.3 1.4 %collective-permute-done.8 = bf16[128,256]{1,0:T(8,128)(2,1)S(1)} collective-permute-done((bf16[128,256]{1,0:T(8,128)(2,1)S(1)}, bf16[128,256]{1,0:T(8,128)(2,1)S(1)}, u32[]{:S(2)}, u32[]{:S(2)}) %collective-permute-start.8) | collective-permute-done | bytes 65568 | tf_op jit(solution)/shard_map/ppermute | solution.py:336
  57.7 5.2 %collective-permute-done.11 = bf16[2,128,256]{2,1,0:T(8,128)(2,1)S(1)} collective-permute-done((bf16[2,128,256]{2,1,0:T(8,128)(2,1)S(1)}, bf16[2,128,256]{2,1,0:T(8,128)(2,1)S(1)}, u32[]{:S(2)}, u32[]{:S(2)}) %collective-permute-start.11) | collective-permute-done | bytes 131104 | tf_op jit(solution)/shard_map/ppermute | solution.py:336
  63.0 2.0 %collective-permute-start.14 = (bf16[128,256]{1,0:T(8,128)(2,1)S(1)}, bf16[128,256]{1,0:T(8,128)(2,1)S(1)}, u32[]{:S(2)}, u32[]{:S(2)}) collective-permute-start(bf16[128,256]{1,0:T(8,128)(2,1)S(1)} %dynamic-slice_bitcast_fusion.3), channel_id=1, source_target_pairs={{0,2},{2,0},{4,6},{6,4},{1,3},{3,1},{5,7},{7,5},{8,10},{10,8},{12,... | collective-permute-start | bytes 196616 | tf_op jit(solution)/shard_map/ppermute | solution.py:336
  65.0 2.4 %collective-permute-done.12 = bf16[128,256]{1,0:T(8,128)(2,1)S(1)} collective-permute-done((bf16[128,256]{1,0:T(8,128)(2,1)S(1)}, bf16[128,256]{1,0:T(8,128)(2,1)S(1)}, u32[]{:S(2)}, u32[]{:S(2)}) %collective-permute-start.12) | collective-permute-done | bytes 65568 | tf_op jit(solution)/shard_map/ppermute | solution.py:336
  68.7 4.2 %collective-permute-done.13 = bf16[128,256]{1,0:T(8,128)(2,1)S(1)} collective-permute-done((bf16[128,256]{1,0:T(8,128)(2,1)S(1)}, bf16[128,256]{1,0:T(8,128)(2,1)S(1)}, u32[]{:S(2)}, u32[]{:S(2)}) %collective-permute-start.13) | collective-permute-done | bytes 65568 | tf_op jit(solution)/shard_map/ppermute | solution.py:336
  73.6 0.9 %collective-permute-start.16 = (bf16[128,256]{1,0:T(8,128)(2,1)S(1)}, bf16[128,256]{1,0:T(8,128)(2,1)S(1)}, u32[]{:S(2)}, u32[]{:S(2)}) collective-permute-start(bf16[128,256]{1,0:T(8,128)(2,1)S(1)} %add_convert_fusion), channel_id=1, source_target_pairs={{0,16},{8,24},{16,0},{24,8},{1,17},{9,25},{17,1},{25,9},{2,18},{10... | collective-permute-start | bytes 196616 | tf_op jit(solution)/shard_map/ppermute | solution.py:336
  74.5 2.0 %collective-permute-start.17 = (bf16[128,256]{1,0:T(8,128)(2,1)S(1)}, bf16[128,256]{1,0:T(8,128)(2,1)S(1)}, u32[]{:S(2)}, u32[]{:S(2)}) collective-permute-start(bf16[128,256]{1,0:T(8,128)(2,1)S(1)} %add_convert_fusion), channel_id=1, source_target_pairs={{0,24},{8,16},{16,8},{24,0},{1,25},{9,17},{17,9},{25,1},{2,26},{10... | collective-permute-start | bytes 196616 | tf_op jit(solution)/shard_map/ppermute | solution.py:336
  77.9 1.8 %collective-permute-done.17 = bf16[128,256]{1,0:T(8,128)(2,1)S(1)} collective-permute-done((bf16[128,256]{1,0:T(8,128)(2,1)S(1)}, bf16[128,256]{1,0:T(8,128)(2,1)S(1)}, u32[]{:S(2)}, u32[]{:S(2)}) %collective-permute-start.17) | collective-permute-done | bytes 65568 | tf_op jit(solution)/shard_map/ppermute | solution.py:336
  79.8 1.1 %row_outputs.1 = (bf16[512,256]{1,0:T(8,128)(2,1)}, bf16[512,256]{1,0:T(8,128)(2,1)}) custom-call(bf16[1536,256]{1,0:T(8,128)(2,1)S(1)} %pad_maximum_fusion.near_ref.packed_ref, bf16[512,256]{1,0:T(8,128)(2,1)S(1)} %get-tuple-element.61.attended_ref, bf16[512,256]{1,0:T(8,128)(2,1)S(1)} %get-tuple-element.62.gquery_ref), custom_call_target="tpu_custom_call" | custom-call | flops 268435456 | bytes 2097152 | tf_op jit(solution)/shard_map/row_outputs/pallas_call | solution.py:397
  81.4 1.0 %slice_bitcast_fusion = (f32[256,256]{1,0:T(8,128)}, f32[256,256]{1,0:T(8,128)}, f32[256,256]{1,0:T(8,128)}, f32[256,256]{1,0:T(8,128)}) fusion(f32[4,256,256]{2,1,0:T(8,128)S(1)} %convert.6), kind=kLoop, calls=%fused_computation.5 | loop fusion | bytes 2097152 | tf_op jit(solution)/shard_map/squeeze | solution.py:572
  (64 shorter events, 9.9 us)
Async XLA Ops:
  0.6 10.0 %copy-start = (bf16[256,256]{1,0:T(8,128)(2,1)S(1)}, bf16[256,256]{1,0:T(8,128)(2,1)}, u32[]{:S(2)}) copy-start(bf16[256,256]{1,0:T(8,128)(2,1)} %param.12) | copy-start | bytes 393220
  0.6 10.0 %copy-start.1 = (bf16[256,256]{1,0:T(8,128)(2,1)S(1)}, bf16[256,256]{1,0:T(8,128)(2,1)}, u32[]{:S(2)}) copy-start(bf16[256,256]{1,0:T(8,128)(2,1)} %param.13) | copy-start | bytes 393220
  0.7 8.0 %collective-permute-start = (bf16[128,256]{1,0:T(8,128)(2,1)}, bf16[128,256]{1,0:T(8,128)(2,1)S(1)}, u32[]{:S(2)}, u32[]{:S(2)}) collective-permute-start(bf16[128,256]{1,0:T(8,128)(2,1)} %bitcast.92), channel_id=1, source_target_pairs={{0,4},{2,6},{4,0},{6,2},{1,5},{3,7},{5,1},{7,3},{8,12},{10,14},{12... | collective-permute-start | bytes 196616 | tf_op jit(solution)/shard_map/ppermute | solution.py:336
  8.6 5.0 %collective-permute-start.1 = (bf16[2,128,256]{2,1,0:T(8,128)(2,1)S(1)}, bf16[2,128,256]{2,1,0:T(8,128)(2,1)S(1)}, u32[]{:S(2)}, u32[]{:S(2)}) collective-permute-start(bf16[2,128,256]{2,1,0:T(8,128)(2,1)S(1)} %bitcast_dynamic-update-slice_fusion.10), channel_id=1, source_target_pairs={{0,2},{2,0},{4,6},{6,4},{1,3},{3,1},{5,7},{7,5},{8,10},{10,8},{12,... | collective-permute-start | bytes 393224 | tf_op jit(solution)/shard_map/ppermute | solution.py:336
  13.7 1.6 %collective-permute-start.2 = (bf16[2,2,128,256]{3,2,1,0:T(8,128)(2,1)S(1)}, bf16[2,2,128,256]{3,2,1,0:T(8,128)(2,1)S(1)}, u32[]{:S(2)}, u32[]{:S(2)}) collective-permute-start(bf16[2,2,128,256]{3,2,1,0:T(8,128)(2,1)S(1)} %bitcast_dynamic-update-slice_fusion.5), channel_id=1, source_target_pairs={{0,1},{1,0},{2,3},{3,2},{4,5},{5,4},{6,7},{7,6},{8,9},{9,8},{10,11... | collective-permute-start | bytes 786440 | tf_op jit(solution)/shard_map/ppermute | solution.py:336
  24.5 4.2 %collective-permute-start.3 = (f32[3,4,1024]{2,1,0:T(4,128)S(1)}, f32[3,4,1024]{2,1,0:T(4,128)S(1)}, u32[]{:S(2)}, u32[]{:S(2)}) collective-permute-start(f32[3,4,1024]{2,1,0:T(4,128)S(1)} %get-tuple-element.53.own_ref), channel_id=1, source_target_pairs={{0,2},{2,0},{4,6},{6,4},{1,3},{3,1},{5,7},{7,5},{8,10},{10,8},{12,... | collective-permute-start | bytes 147464 | tf_op jit(solution)/shard_map/ppermute | solution.py:336
  28.7 5.1 %collective-permute-start.4 = (f32[3,4,1024]{2,1,0:T(4,128)S(1)}, f32[3,4,1024]{2,1,0:T(4,128)S(1)}, u32[]{:S(2)}, u32[]{:S(2)}) collective-permute-start(f32[3,4,1024]{2,1,0:T(4,128)S(1)} %pad_maximum_fusion.1), channel_id=1, source_target_pairs={{0,4},{2,6},{4,0},{6,2},{1,5},{3,7},{5,1},{7,3},{8,12},{10,14},{12... | collective-permute-start | bytes 147464 | tf_op jit(solution)/shard_map/ppermute | solution.py:336
  33.8 1.3 %collective-permute-start.5 = (f32[3,4,1024]{2,1,0:T(4,128)S(1)}, f32[3,4,1024]{2,1,0:T(4,128)S(1)}, u32[]{:S(2)}, u32[]{:S(2)}) collective-permute-start(f32[3,4,1024]{2,1,0:T(4,128)S(1)} %pad_maximum_fusion.2.near_ref), channel_id=1, source_target_pairs={{0,1},{1,0},{2,3},{3,2},{4,5},{5,4},{6,7},{7,6},{8,9},{9,8},{10,11... | collective-permute-start | bytes 147464 | tf_op jit(solution)/shard_map/ppermute | solution.py:336
  46.7 1.6 %collective-permute-start.7 = (bf16[2,2,128,256]{3,2,1,0:T(8,128)(2,1)S(1)}, bf16[2,2,128,256]{3,2,1,0:T(8,128)(2,1)S(1)}, u32[]{:S(2)}, u32[]{:S(2)}) collective-permute-start(bf16[2,2,128,256]{3,2,1,0:T(8,128)(2,1)S(1)} %dynamic-slice_bitcast_fusion), channel_id=1, source_target_pairs={{0,1},{1,0},{2,3},{3,2},{4,5},{5,4},{6,7},{7,6},{8,9},{9,8},{10,11... | collective-permute-start | bytes 786440 | tf_op jit(solution)/shard_map/ppermute | solution.py:336
  46.8 1.9 %collective-permute-start.6 = (bf16[2,2,128,256]{3,2,1,0:T(8,128)(2,1)S(1)}, bf16[2,2,128,256]{3,2,1,0:T(8,128)(2,1)S(1)}, u32[]{:S(2)}, u32[]{:S(2)}) collective-permute-start(bf16[2,2,128,256]{3,2,1,0:T(8,128)(2,1)S(1)} %dynamic-slice_bitcast_fusion.1), channel_id=1, source_target_pairs={{0,1},{1,0},{2,3},{3,2},{4,5},{5,4},{6,7},{7,6},{8,9},{9,8},{10,11... | collective-permute-start | bytes 786440 | tf_op jit(solution)/shard_map/ppermute | solution.py:336
  48.8 7.5 %collective-permute-start.10 = (bf16[128,256]{1,0:T(8,128)(2,1)S(1)}, bf16[128,256]{1,0:T(8,128)(2,1)S(1)}, u32[]{:S(2)}, u32[]{:S(2)}) collective-permute-start(bf16[128,256]{1,0:T(8,128)(2,1)S(1)} %get-tuple-element.76), channel_id=1, source_target_pairs={{0,24},{8,16},{16,8},{24,0},{1,25},{9,17},{17,9},{25,1},{2,26},{10... | collective-permute-start | bytes 196616 | tf_op jit(solution)/shard_map/ppermute | solution.py:336
  53.4 4.3 %collective-permute-start.8 = (bf16[128,256]{1,0:T(8,128)(2,1)S(1)}, bf16[128,256]{1,0:T(8,128)(2,1)S(1)}, u32[]{:S(2)}, u32[]{:S(2)}) collective-permute-start(bf16[128,256]{1,0:T(8,128)(2,1)S(1)} %get-tuple-element.75), channel_id=1, source_target_pairs={{0,8},{8,0},{16,24},{24,16},{1,9},{9,1},{17,25},{25,17},{2,10},{10... | collective-permute-start | bytes 196616 | tf_op jit(solution)/shard_map/ppermute | solution.py:336
  53.4 4.3 %collective-permute-start.9 = (bf16[128,256]{1,0:T(8,128)(2,1)S(1)}, bf16[128,256]{1,0:T(8,128)(2,1)S(1)}, u32[]{:S(2)}, u32[]{:S(2)}) collective-permute-start(bf16[128,256]{1,0:T(8,128)(2,1)S(1)} %get-tuple-element.77), channel_id=1, source_target_pairs={{0,16},{8,24},{16,0},{24,8},{1,17},{9,25},{17,1},{25,9},{2,18},{10... | collective-permute-start | bytes 196616 | tf_op jit(solution)/shard_map/ppermute | solution.py:336
  54.0 8.8 %collective-permute-start.11 = (bf16[2,128,256]{2,1,0:T(8,128)(2,1)S(1)}, bf16[2,128,256]{2,1,0:T(8,128)(2,1)S(1)}, u32[]{:S(2)}, u32[]{:S(2)}) collective-permute-start(bf16[2,128,256]{2,1,0:T(8,128)(2,1)S(1)} %dynamic-slice_bitcast_fusion.2), channel_id=1, source_target_pairs={{0,4},{2,6},{4,0},{6,2},{1,5},{3,7},{5,1},{7,3},{8,12},{10,14},{12... | collective-permute-start | bytes 393224 | tf_op jit(solution)/shard_map/ppermute | solution.py:336
  62.9 4.5 %collective-permute-start.12 = (bf16[128,256]{1,0:T(8,128)(2,1)S(1)}, bf16[128,256]{1,0:T(8,128)(2,1)S(1)}, u32[]{:S(2)}, u32[]{:S(2)}) collective-permute-start(bf16[128,256]{1,0:T(8,128)(2,1)S(1)} %fusion.6), channel_id=1, source_target_pairs={{0,2},{2,0},{4,6},{6,4},{1,3},{3,1},{5,7},{7,5},{8,10},{10,8},{12,... | collective-permute-start | bytes 196616 | tf_op jit(solution)/shard_map/ppermute | solution.py:336
  63.0 5.1 %collective-permute-start.14 = (bf16[128,256]{1,0:T(8,128)(2,1)S(1)}, bf16[128,256]{1,0:T(8,128)(2,1)S(1)}, u32[]{:S(2)}, u32[]{:S(2)}) collective-permute-start(bf16[128,256]{1,0:T(8,128)(2,1)S(1)} %dynamic-slice_bitcast_fusion.3), channel_id=1, source_target_pairs={{0,2},{2,0},{4,6},{6,4},{1,3},{3,1},{5,7},{7,5},{8,10},{10,8},{12,... | collective-permute-start | bytes 196616 | tf_op jit(solution)/shard_map/ppermute | solution.py:336
  67.4 5.6 %collective-permute-start.13 = (bf16[128,256]{1,0:T(8,128)(2,1)S(1)}, bf16[128,256]{1,0:T(8,128)(2,1)S(1)}, u32[]{:S(2)}, u32[]{:S(2)}) collective-permute-start(bf16[128,256]{1,0:T(8,128)(2,1)S(1)} %add_convert_fusion.1), channel_id=1, source_target_pairs={{0,4},{2,6},{4,0},{6,2},{1,5},{3,7},{5,1},{7,3},{8,12},{10,14},{12... | collective-permute-start | bytes 196616 | tf_op jit(solution)/shard_map/ppermute | solution.py:336
  73.0 4.3 %collective-permute-start.15 = (bf16[128,256]{1,0:T(8,128)(2,1)S(1)}, bf16[128,256]{1,0:T(8,128)(2,1)S(1)}, u32[]{:S(2)}, u32[]{:S(2)}) collective-permute-start(bf16[128,256]{1,0:T(8,128)(2,1)S(1)} %add_convert_fusion), channel_id=1, source_target_pairs={{0,8},{8,0},{16,24},{24,16},{1,9},{9,1},{17,25},{25,17},{2,10},{10... | collective-permute-start | bytes 196616 | tf_op jit(solution)/shard_map/ppermute | solution.py:336
  73.6 4.3 %collective-permute-start.16 = (bf16[128,256]{1,0:T(8,128)(2,1)S(1)}, bf16[128,256]{1,0:T(8,128)(2,1)S(1)}, u32[]{:S(2)}, u32[]{:S(2)}) collective-permute-start(bf16[128,256]{1,0:T(8,128)(2,1)S(1)} %add_convert_fusion), channel_id=1, source_target_pairs={{0,16},{8,24},{16,0},{24,8},{1,17},{9,25},{17,1},{25,9},{2,18},{10... | collective-permute-start | bytes 196616 | tf_op jit(solution)/shard_map/ppermute | solution.py:336
  74.5 5.2 %collective-permute-start.17 = (bf16[128,256]{1,0:T(8,128)(2,1)S(1)}, bf16[128,256]{1,0:T(8,128)(2,1)S(1)}, u32[]{:S(2)}, u32[]{:S(2)}) collective-permute-start(bf16[128,256]{1,0:T(8,128)(2,1)S(1)} %add_convert_fusion), channel_id=1, source_target_pairs={{0,24},{8,16},{16,8},{24,0},{1,25},{9,17},{17,9},{25,1},{2,26},{10... | collective-permute-start | bytes 196616 | tf_op jit(solution)/shard_map/ppermute | solution.py:336
  79.7 1.6 %collective-permute-start.18 = (bf16[4,128,256]{2,1,0:T(8,128)(2,1)S(1)}, bf16[4,128,256]{2,1,0:T(8,128)(2,1)S(1)}, u32[]{:S(2)}, u32[]{:S(2)}) collective-permute-start(bf16[4,128,256]{2,1,0:T(8,128)(2,1)S(1)} %bitcast_dynamic-update-slice_fusion.6), channel_id=1, source_target_pairs={{0,1},{1,0},{2,3},{3,2},{4,5},{5,4},{6,7},{7,6},{8,9},{9,8},{10,11... | collective-permute-start | bytes 786440 | tf_op jit(solution)/shard_map/ppermute | solution.py:336
where the time goes:
time: 81.9 us; the launch traced here: 82.4 us
  waiting for transfers between devices  33.9 us (41%)
  Pallas kernels  22.8 us (28%)
  starting transfers between devices  19.5 us (24%)
  other arithmetic  2.98 us (4%)
  local copies, waits for them, and re-layouts  2.25 us (3%)
  between operations  0.96 us (1%)
    ppermute x19, waiting for transfers between devices, swap(): return lax.ppermute(x, axis, pairs)  33.9 us
    pallas_call x6, Pallas kernels, vmem_call(): pl.pallas_call(kernel, name=name, out_shape=out_shape, in_specs=specs, ou...  22.8 us
    ppermute x19, starting transfers between devices, swap(): return lax.ppermute(x, axis, pairs)  19.5 us
  transfers between devices with their start and end apart: 19, of which 18 were waited for; matrix products, arithmetic and copies ran while one was open for 5% of the time, Pallas kernels for 3%

commit v1 on v0

--- a/solution.py
+++ b/solution.py
@@ -207,16 +207,12 @@
     key_ref[...] = bf(mm(src_ref[...], wk_ref[...]))
     value_ref[...] = bf(mm(src_ref[...], wv_ref[...]))
     query_t = bf(mm_general(wq_ref[...], ref_ref[...], TT)).astype(jnp.float32)
-    query_t = bf(query_t * (2.0 * head_dim ** -0.5))
-    grad_t = bf(mm_general(wo_ref[...], gout_ref[...], NT))
-    for values, out_ref in ((query_t, query_t_ref), (grad_t, grad_t_ref)):
-        out_ref[...] = jnp.zeros(out_ref.shape, jnp.bfloat16)
-        for query_block in range(rows // BLOCK):
-            span = slice(query_block * BLOCK, (query_block + 1) * BLOCK)
-            for head in range(heads):
-                mine = slice(head * head_dim, (head + 1) * head_dim)
-                lanes = slice(head * BLOCK, (head + 1) * BLOCK)
-                out_ref[query_block, mine, lanes] = values[mine, span]
+    query_t = query_t * (2.0 * head_dim ** -0.5)
+    grad_t = mm_general(wo_ref[...], gout_ref[...], NT)
+    for query_block in range(rows // BLOCK):
+        span = slice(query_block * BLOCK, (query_block + 1) * BLOCK)
+        query_t_ref[query_block] = bf(query_t[:, span])
+        grad_t_ref[query_block] = bf(grad_t[:, span])
 
 
 def grads_kernel(
@@ -271,12 +267,15 @@
                 dot_ref[span, :] = row_dot.reshape(STRIP, 128)
 
     def own_lanes(stacked):
-        total = None
-        for head in range(heads):
-            own = lane_row(width, head, head_dim).astype(jnp.float32)
-            piece = stacked[head * BLOCK : (head + 1) * BLOCK] * own
-            total = piece if total is None else total + piece
-        return total
+        lane = lax.broadcasted_iota(jnp.int32, (BLOCK, 128), 1)
+        tiles_out = []
+        for first in range(0, width, 128):
+            out = None
+            for head in range(first // head_dim, (first + 128) // head_dim):
+                piece = stacked[head * BLOCK : (head + 1) * BLOCK, first : first + 128]
+                out = piece if out is None else jnp.where(lane < head * head_dim - first, out, piece)
+            tiles_out.append(out)
+        return jnp.concatenate(tiles_out, axis=1)
 
     def outputs(query_block, step, listed):
         score_now, rest_now, match_now = [
@@ -292,8 +291,11 @@
         span = pl.ds(pl.multiple_of(step * STEP, STEP), STEP)
         att_ref[query_block] += own_lanes(mm(match_now[...], value_ref[span, :]))
         gq_ref[query_block] += own_lanes(mm(gscore_ref[...], key_ref[span, :]))
-        gk_ref[step] += mm(query_t_ref[query_block], gscore_ref[...])
-        gv_ref[step] += mm(grad_t_ref[query_block], match_now[...])
+        for head in range(heads):
+            mine = slice(head * head_dim, (head + 1) * head_dim)
+            rows_of = slice(head * BLOCK, (head + 1) * BLOCK)
+            gk_ref[step, mine, :] += mm(query_t_ref[query_block, mine, :], gscore_ref[rows_of, :])
+            gv_ref[step, mine, :] += mm(grad_t_ref[query_block, mine, :], match_now[rows_of, :])
 
     def query_rows(query_block, carry):
         dot_ref[...] = jnp.zeros(dot_ref.shape, jnp.float32)
@@ -481,8 +483,8 @@
         [
             shape((key_total, width), b16),
             shape((key_total, width), b16),
-            shape((query_blocks, width, stacked), b16),
-            shape((query_blocks, width, stacked), b16),
+            shape((query_blocks, width, BLOCK), b16),
+            shape((query_blocks, width, BLOCK), b16),
         ],
         [],
         8 << 20,
@@ -535,12 +537,12 @@
     scans = lax.axis_size("scan")
     weights = weight_part.reshape((2, scans // 2, 2, -1, width))
     sources = source_part.reshape((2,) * (len(chip_steps) + 1) + (key_rows, width))
-    source_steps = chip_steps[::-1]
+    source_steps = list(zip(chip_steps, range(len(chip_steps) - 1, -1, -1)))
     weights = halve(weights, core_step)
     sources = halve(sources, core_step, len(chip_steps))
     weights, sources = lax.optimization_barrier((weights, sources))
     weights = scatter_direct(weights.reshape((scans,) + weights.shape[2:]), "scan")
-    sources = halve(sources, source_steps[0])
+    sources = halve(sources, *source_steps[0])
     weights, sources, attended, grad_query = lax.optimization_barrier(
         (weights, sources, attended, grad_query)
     )
@@ -555,7 +557,7 @@
         (near_pack, attended, grad_query),
     )
     for step in source_steps[1:]:
-        sources = halve(sources, step)
+        sources = halve(sources, *step)
     for mesh_axis, bit, _ in chip_steps:
         weights = add(weights, swap(weights, mesh_axis, bit))
     weights, grad_src = lax.optimization_barrier((weights, sources))

time: 81.9 us -> 77.3 us (0.944)
  waiting for transfers between devices: 33.9 us -> 25.2 us
  starting transfers between devices: 19.5 us -> 27 us
  Pallas kernels: 22.8 us -> 19.3 us
    ppermute x19, waiting for transfers between devices: 33.9 us -> 25.2 us  [swap(): return lax.ppermute(x, axis, pairs)]
    ppermute x19, starting transfers between devices: 19.5 us -> 27 us  [swap(): return lax.ppermute(x, axis, pairs)]
    pallas_call x6, Pallas kernels: 22.8 us -> 19.3 us  [vmem_call(): pl.pallas_call(kernel, name=name, out_shape=out_shape, in_specs=specs, ou...]
  transfers between devices with their start and end apart: 19 -> 19, of which waited for: 18 -> 16; matrix products, arithmetic and copies ran while one was open for 5% -> 5% of each run, Pallas kernels for 3% -> 3%
where the time goes in v1:
time: 77.3 us; the launch traced here: 77.6 us
  starting transfers between devices  27 us (35%)
  waiting for transfers between devices  25.2 us (33%)
  Pallas kernels  19.3 us (25%)
  other arithmetic  2.99 us (4%)
  local copies, waits for them, and re-layouts  2.28 us (3%)
  between operations  0.95 us (1%)
    ppermute x19, starting transfers between devices, swap(): return lax.ppermute(x, axis, pairs)  27 us
    ppermute x19, waiting for transfers between devices, swap(): return lax.ppermute(x, axis, pairs)  25.2 us
    pallas_call x6, Pallas kernels, vmem_call(): pl.pallas_call(kernel, name=name, out_shape=out_shape, in_specs=specs, ou...  19.3 us
  transfers between devices with their start and end apart: 19, of which 16 were waited for; matrix products, arithmetic and copies ran while one was open for 5% of the time, Pallas kernels for 3%

profile of v1, /device:TPU:0, one launch (start us, length us, event | category | flops | bytes accessed | tf_op | source)
XLA Modules:
  0.0 77.6 jit_solution(9125349879245245326)
XLA Ops:
  0.7 4.1 %collective-permute-start = (bf16[128,256]{1,0:T(8,128)(2,1)}, bf16[128,256]{1,0:T(8,128)(2,1)S(1)}, u32[]{:S(2)}, u32[]{:S(2)}) collective-permute-start(bf16[128,256]{1,0:T(8,128)(2,1)} %bitcast.93), channel_id=1, source_target_pairs={{0,4},{2,6},{4,0},{6,2},{1,5},{3,7},{5,1},{7,3},{8,12},{10,14},{12... | collective-permute-start | bytes 196616 | tf_op jit(solution)/shard_map/ppermute | solution.py:338
  6.3 2.3 %collective-permute-done = bf16[128,256]{1,0:T(8,128)(2,1)S(1)} collective-permute-done((bf16[128,256]{1,0:T(8,128)(2,1)}, bf16[128,256]{1,0:T(8,128)(2,1)S(1)}, u32[]{:S(2)}, u32[]{:S(2)}) %collective-permute-start) | collective-permute-done | bytes 65568 | tf_op jit(solution)/shard_map/ppermute | solution.py:338
  9.4 1.2 %pad_maximum_fusion.near_ref.packed_ref = bf16[1536,256]{1,0:T(8,128)(2,1)S(1)} fusion(bf16[256,256]{1,0:T(8,128)(2,1)} %param.14, bf16[256,256]{1,0:T(8,128)(2,1)} %param.11, bf16[512,256]{1,0:T(8,128)(2,1)} %bitcast.90, bf16[512,256]{1,0:T(8,128)(2,1)} %bitcast.91), kind=kLoop, calls=%fused_computation | loop fusion | flops 3145728 | bytes 1572864 | tf_op jit(solution)/shard_map/concatenate | solution.py:428
  10.7 3.0 %collective-permute-done.1 = bf16[2,128,256]{2,1,0:T(8,128)(2,1)S(1)} collective-permute-done((bf16[2,128,256]{2,1,0:T(8,128)(2,1)S(1)}, bf16[2,128,256]{2,1,0:T(8,128)(2,1)S(1)}, u32[]{:S(2)}, u32[]{:S(2)}) %collective-permute-start.1) | collective-permute-done | bytes 131104 | tf_op jit(solution)/shard_map/ppermute | solution.py:338
  14.2 1.1 %collective-permute-done.2 = bf16[2,2,128,256]{3,2,1,0:T(8,128)(2,1)S(1)} collective-permute-done((bf16[2,2,128,256]{3,2,1,0:T(8,128)(2,1)S(1)}, bf16[2,2,128,256]{3,2,1,0:T(8,128)(2,1)S(1)}, u32[]{:S(2)}, u32[]{:S(2)}) %collective-permute-start.2) | collective-permute-done | bytes 262176 | tf_op jit(solution)/shard_map/ppermute | solution.py:338
  15.3 8.0 %match_stats.1 = (f32[4,512,128]{2,1,0:T(8,128)S(1)}, f32[4,512,128]{2,1,0:T(8,128)S(1)}, f32[3,4,1024]{2,1,0:T(4,128)S(1)}, f32[16,512,256]{2,1,0:T(8,128)S(1)}, bf16[16,512,256]{2,1,0:T(8,128)(2,1)S(1)}) custom-call(s32[4,8]{1,0:T(4,128)S(1)} %select_bitcast_fusion.inter_ref, bf16[4,512,256]{2,1,0:T(8,128)(2,1)S(1)} %get-tuple-element.40.left_ref, ...), custom_call_target="tpu_custom_call" | custom-call | flops 4026531840 | bytes 8388608 | tf_op jit(solution)/shard_map/match_stats/pallas_call | solution.py:399
  23.5 4.2 %collective-permute-done.3 = f32[3,4,1024]{2,1,0:T(4,128)S(1)} collective-permute-done((f32[3,4,1024]{2,1,0:T(4,128)S(1)}, f32[3,4,1024]{2,1,0:T(4,128)S(1)}, u32[]{:S(2)}, u32[]{:S(2)}) %collective-permute-start.3) | collective-permute-done | bytes 49184 | tf_op jit(solution)/shard_map/ppermute | solution.py:338
  27.8 3.6 %collective-permute-start.4 = (f32[3,4,1024]{2,1,0:T(4,128)S(1)}, f32[3,4,1024]{2,1,0:T(4,128)S(1)}, u32[]{:S(2)}, u32[]{:S(2)}) collective-permute-start(f32[3,4,1024]{2,1,0:T(4,128)S(1)} %pad_maximum_fusion.1), channel_id=1, source_target_pairs={{0,4},{2,6},{4,0},{6,2},{1,5},{3,7},{5,1},{7,3},{8,12},{10,14},{12... | collective-permute-start | bytes 147464 | tf_op jit(solution)/shard_map/ppermute | solution.py:338
  31.4 2.1 %collective-permute-done.4 = f32[3,4,1024]{2,1,0:T(4,128)S(1)} collective-permute-done((f32[3,4,1024]{2,1,0:T(4,128)S(1)}, f32[3,4,1024]{2,1,0:T(4,128)S(1)}, u32[]{:S(2)}, u32[]{:S(2)}) %collective-permute-start.4) | collective-permute-done | bytes 49184 | tf_op jit(solution)/shard_map/ppermute | solution.py:338
  34.8 8.7 %match_grads.1 = (bf16[512,256]{1,0:T(8,128)(2,1)S(1)}, bf16[512,256]{1,0:T(8,128)(2,1)S(1)}, bf16[256,1024]{1,0:T(8,128)(2,1)S(1)}, bf16[256,1024]{1,0:T(8,128)(2,1)S(1)}, bf16[4,256,256]{2,1,0:T(8,128)(2,1)S(1)}) custom-call(s32[4,8]{1,0:T(4,128)S(1)} %select_bitcast_fusion.inter_ref, f32[16,512,256]{2,1,0:T(8,128)S(1)} %get-tuple-element.45.score_ref, ...), custom_call_target="tpu_custom_call" | custom-call | flops 6710886400 | bytes 8388608 | tf_op jit(solution)/shard_map/match_grads/pallas_call | solution.py:399
  46.8 2.4 %collective-permute-start.8 = (bf16[128,256]{1,0:T(8,128)(2,1)S(1)}, bf16[128,256]{1,0:T(8,128)(2,1)S(1)}, u32[]{:S(2)}, u32[]{:S(2)}) collective-permute-start(bf16[128,256]{1,0:T(8,128)(2,1)S(1)} %get-tuple-element.77), channel_id=1, source_target_pairs={{0,8},{8,0},{16,24},{24,16},{1,9},{9,1},{17,25},{25,17},{2,10},{10... | collective-permute-start | bytes 196616 | tf_op jit(solution)/shard_map/ppermute | solution.py:338
  49.3 1.0 %collective-permute-start.9 = (bf16[128,256]{1,0:T(8,128)(2,1)S(1)}, bf16[128,256]{1,0:T(8,128)(2,1)S(1)}, u32[]{:S(2)}, u32[]{:S(2)}) collective-permute-start(bf16[128,256]{1,0:T(8,128)(2,1)S(1)} %get-tuple-element.79), channel_id=1, source_target_pairs={{0,16},{8,24},{16,0},{24,8},{1,17},{9,25},{17,1},{25,9},{2,18},{10... | collective-permute-start | bytes 196616 | tf_op jit(solution)/shard_map/ppermute | solution.py:338
  50.3 3.9 %collective-permute-start.11 = (bf16[2,128,256]{2,1,0:T(8,128)(2,1)S(1)}, bf16[2,128,256]{2,1,0:T(8,128)(2,1)S(1)}, u32[]{:S(2)}, u32[]{:S(2)}) collective-permute-start(bf16[2,128,256]{2,1,0:T(8,128)(2,1)S(1)} %dynamic-slice_bitcast_fusion.1), channel_id=1, source_target_pairs={{0,2},{2,0},{4,6},{6,4},{1,3},{3,1},{5,7},{7,5},{8,10},{10,8},{12,... | collective-permute-start | bytes 393224 | tf_op jit(solution)/shard_map/ppermute | solution.py:338
  54.3 3.4 %collective-permute-done.11 = bf16[2,128,256]{2,1,0:T(8,128)(2,1)S(1)} collective-permute-done((bf16[2,128,256]{2,1,0:T(8,128)(2,1)S(1)}, bf16[2,128,256]{2,1,0:T(8,128)(2,1)S(1)}, u32[]{:S(2)}, u32[]{:S(2)}) %collective-permute-start.11) | collective-permute-done | bytes 131104 | tf_op jit(solution)/shard_map/ppermute | solution.py:338
  57.7 1.8 %collective-permute-start.12 = (bf16[128,256]{1,0:T(8,128)(2,1)S(1)}, bf16[128,256]{1,0:T(8,128)(2,1)S(1)}, u32[]{:S(2)}, u32[]{:S(2)}) collective-permute-start(bf16[128,256]{1,0:T(8,128)(2,1)S(1)} %fusion.6), channel_id=1, source_target_pairs={{0,2},{2,0},{4,6},{6,4},{1,3},{3,1},{5,7},{7,5},{8,10},{10,8},{12,... | collective-permute-start | bytes 196616 | tf_op jit(solution)/shard_map/ppermute | solution.py:338
  59.5 2.2 %collective-permute-start.14 = (bf16[128,256]{1,0:T(8,128)(2,1)S(1)}, bf16[128,256]{1,0:T(8,128)(2,1)S(1)}, u32[]{:S(2)}, u32[]{:S(2)}) collective-permute-start(bf16[128,256]{1,0:T(8,128)(2,1)S(1)} %dynamic-slice_bitcast_fusion.2), channel_id=1, source_target_pairs={{0,4},{2,6},{4,0},{6,2},{1,5},{3,7},{5,1},{7,3},{8,12},{10,14},{12... | collective-permute-start | bytes 196616 | tf_op jit(solution)/shard_map/ppermute | solution.py:338
  62.2 2.1 %collective-permute-start.13 = (bf16[128,256]{1,0:T(8,128)(2,1)S(1)}, bf16[128,256]{1,0:T(8,128)(2,1)S(1)}, u32[]{:S(2)}, u32[]{:S(2)}) collective-permute-start(bf16[128,256]{1,0:T(8,128)(2,1)S(1)} %add_convert_fusion.1), channel_id=1, source_target_pairs={{0,4},{2,6},{4,0},{6,2},{1,5},{3,7},{5,1},{7,3},{8,12},{10,14},{12... | collective-permute-start | bytes 196616 | tf_op jit(solution)/shard_map/ppermute | solution.py:338
  64.3 2.2 %collective-permute-done.14 = bf16[128,256]{1,0:T(8,128)(2,1)S(1)} collective-permute-done((bf16[128,256]{1,0:T(8,128)(2,1)S(1)}, bf16[128,256]{1,0:T(8,128)(2,1)S(1)}, u32[]{:S(2)}, u32[]{:S(2)}) %collective-permute-start.14) | collective-permute-done | bytes 65568 | tf_op jit(solution)/shard_map/ppermute | solution.py:338
  68.2 1.6 %collective-permute-start.16 = (bf16[128,256]{1,0:T(8,128)(2,1)S(1)}, bf16[128,256]{1,0:T(8,128)(2,1)S(1)}, u32[]{:S(2)}, u32[]{:S(2)}) collective-permute-start(bf16[128,256]{1,0:T(8,128)(2,1)S(1)} %add_convert_fusion), channel_id=1, source_target_pairs={{0,16},{8,24},{16,0},{24,8},{1,17},{9,25},{17,1},{25,9},{2,18},{10... | collective-permute-start | bytes 196616 | tf_op jit(solution)/shard_map/ppermute | solution.py:338
  69.7 1.4 %collective-permute-start.17 = (bf16[128,256]{1,0:T(8,128)(2,1)S(1)}, bf16[128,256]{1,0:T(8,128)(2,1)S(1)}, u32[]{:S(2)}, u32[]{:S(2)}) collective-permute-start(bf16[128,256]{1,0:T(8,128)(2,1)S(1)} %add_convert_fusion), channel_id=1, source_target_pairs={{0,24},{8,16},{16,8},{24,0},{1,25},{9,17},{17,9},{25,1},{2,26},{10... | collective-permute-start | bytes 196616 | tf_op jit(solution)/shard_map/ppermute | solution.py:338
  71.1 1.1 %collective-permute-done.15 = bf16[128,256]{1,0:T(8,128)(2,1)S(1)} collective-permute-done((bf16[128,256]{1,0:T(8,128)(2,1)S(1)}, bf16[128,256]{1,0:T(8,128)(2,1)S(1)}, u32[]{:S(2)}, u32[]{:S(2)}) %collective-permute-start.15) | collective-permute-done | bytes 65568 | tf_op jit(solution)/shard_map/ppermute | solution.py:338
  73.1 1.8 %collective-permute-done.17 = bf16[128,256]{1,0:T(8,128)(2,1)S(1)} collective-permute-done((bf16[128,256]{1,0:T(8,128)(2,1)S(1)}, bf16[128,256]{1,0:T(8,128)(2,1)S(1)}, u32[]{:S(2)}, u32[]{:S(2)}) %collective-permute-start.17) | collective-permute-done | bytes 65568 | tf_op jit(solution)/shard_map/ppermute | solution.py:338
  75.0 1.1 %row_outputs.1 = (bf16[512,256]{1,0:T(8,128)(2,1)}, bf16[512,256]{1,0:T(8,128)(2,1)}) custom-call(bf16[1536,256]{1,0:T(8,128)(2,1)S(1)} %pad_maximum_fusion.near_ref.packed_ref, bf16[512,256]{1,0:T(8,128)(2,1)S(1)} %get-tuple-element.61.attended_ref, bf16[512,256]{1,0:T(8,128)(2,1)S(1)} %get-tuple-element.62.gquery_ref), custom_call_target="tpu_custom_call" | custom-call | flops 268435456 | bytes 2097152 | tf_op jit(solution)/shard_map/row_outputs/pallas_call | solution.py:399
  76.6 1.0 %slice_bitcast_fusion = (f32[256,256]{1,0:T(8,128)}, f32[256,256]{1,0:T(8,128)}, f32[256,256]{1,0:T(8,128)}, f32[256,256]{1,0:T(8,128)}) fusion(f32[4,256,256]{2,1,0:T(8,128)S(1)} %convert.6), kind=kLoop, calls=%fused_computation.5 | loop fusion | bytes 2097152 | tf_op jit(solution)/shard_map/squeeze | solution.py:574
  (65 shorter events, 11.3 us)
Async XLA Ops:
  0.6 10.0 %copy-start = (bf16[256,256]{1,0:T(8,128)(2,1)S(1)}, bf16[256,256]{1,0:T(8,128)(2,1)}, u32[]{:S(2)}) copy-start(bf16[256,256]{1,0:T(8,128)(2,1)} %param.12) | copy-start | bytes 393220
  0.6 10.0 %copy-start.1 = (bf16[256,256]{1,0:T(8,128)(2,1)S(1)}, bf16[256,256]{1,0:T(8,128)(2,1)}, u32[]{:S(2)}) copy-start(bf16[256,256]{1,0:T(8,128)(2,1)} %param.13) | copy-start | bytes 393220
  0.7 8.0 %collective-permute-start = (bf16[128,256]{1,0:T(8,128)(2,1)}, bf16[128,256]{1,0:T(8,128)(2,1)S(1)}, u32[]{:S(2)}, u32[]{:S(2)}) collective-permute-start(bf16[128,256]{1,0:T(8,128)(2,1)} %bitcast.93), channel_id=1, source_target_pairs={{0,4},{2,6},{4,0},{6,2},{1,5},{3,7},{5,1},{7,3},{8,12},{10,14},{12... | collective-permute-start | bytes 196616 | tf_op jit(solution)/shard_map/ppermute | solution.py:338
  8.6 5.0 %collective-permute-start.1 = (bf16[2,128,256]{2,1,0:T(8,128)(2,1)S(1)}, bf16[2,128,256]{2,1,0:T(8,128)(2,1)S(1)}, u32[]{:S(2)}, u32[]{:S(2)}) collective-permute-start(bf16[2,128,256]{2,1,0:T(8,128)(2,1)S(1)} %bitcast_dynamic-update-slice_fusion.10), channel_id=1, source_target_pairs={{0,2},{2,0},{4,6},{6,4},{1,3},{3,1},{5,7},{7,5},{8,10},{10,8},{12,... | collective-permute-start | bytes 393224 | tf_op jit(solution)/shard_map/ppermute | solution.py:338
  13.7 1.6 %collective-permute-start.2 = (bf16[2,2,128,256]{3,2,1,0:T(8,128)(2,1)S(1)}, bf16[2,2,128,256]{3,2,1,0:T(8,128)(2,1)S(1)}, u32[]{:S(2)}, u32[]{:S(2)}) collective-permute-start(bf16[2,2,128,256]{3,2,1,0:T(8,128)(2,1)S(1)} %bitcast_dynamic-update-slice_fusion.5), channel_id=1, source_target_pairs={{0,1},{1,0},{2,3},{3,2},{4,5},{5,4},{6,7},{7,6},{8,9},{9,8},{10,11... | collective-permute-start | bytes 786440 | tf_op jit(solution)/shard_map/ppermute | solution.py:338
  23.3 4.4 %collective-permute-start.3 = (f32[3,4,1024]{2,1,0:T(4,128)S(1)}, f32[3,4,1024]{2,1,0:T(4,128)S(1)}, u32[]{:S(2)}, u32[]{:S(2)}) collective-permute-start(f32[3,4,1024]{2,1,0:T(4,128)S(1)} %get-tuple-element.53.own_ref), channel_id=1, source_target_pairs={{0,2},{2,0},{4,6},{6,4},{1,3},{3,1},{5,7},{7,5},{8,10},{10,8},{12,... | collective-permute-start | bytes 147464 | tf_op jit(solution)/shard_map/ppermute | solution.py:338
  27.8 5.7 %collective-permute-start.4 = (f32[3,4,1024]{2,1,0:T(4,128)S(1)}, f32[3,4,1024]{2,1,0:T(4,128)S(1)}, u32[]{:S(2)}, u32[]{:S(2)}) collective-permute-start(f32[3,4,1024]{2,1,0:T(4,128)S(1)} %pad_maximum_fusion.1), channel_id=1, source_target_pairs={{0,4},{2,6},{4,0},{6,2},{1,5},{3,7},{5,1},{7,3},{8,12},{10,14},{12... | collective-permute-start | bytes 147464 | tf_op jit(solution)/shard_map/ppermute | solution.py:338
  33.5 1.3 %collective-permute-start.5 = (f32[3,4,1024]{2,1,0:T(4,128)S(1)}, f32[3,4,1024]{2,1,0:T(4,128)S(1)}, u32[]{:S(2)}, u32[]{:S(2)}) collective-permute-start(f32[3,4,1024]{2,1,0:T(4,128)S(1)} %pad_maximum_fusion.2.near_ref), channel_id=1, source_target_pairs={{0,1},{1,0},{2,3},{3,2},{4,5},{5,4},{6,7},{7,6},{8,9},{9,8},{10,11... | collective-permute-start | bytes 147464 | tf_op jit(solution)/shard_map/ppermute | solution.py:338
  43.6 2.0 %collective-permute-start.6 = (bf16[2,2,128,256]{3,2,1,0:T(8,128)(2,1)S(1)}, bf16[2,2,128,256]{3,2,1,0:T(8,128)(2,1)S(1)}, u32[]{:S(2)}, u32[]{:S(2)}) collective-permute-start(bf16[2,2,128,256]{3,2,1,0:T(8,128)(2,1)S(1)} %dynamic-slice_bitcast_fusion), channel_id=1, source_target_pairs={{0,1},{1,0},{2,3},{3,2},{4,5},{5,4},{6,7},{7,6},{8,9},{9,8},{10,11... | collective-permute-start | bytes 786440 | tf_op jit(solution)/shard_map/ppermute | solution.py:338
  45.0 1.6 %collective-permute-start.7 = (bf16[2,2,128,256]{3,2,0,1:T(8,128)(2,1)S(1)}, bf16[2,2,128,256]{3,2,0,1:T(8,128)(2,1)S(1)}, u32[]{:S(2)}, u32[]{:S(2)}) collective-permute-start(bf16[2,2,128,256]{3,2,0,1:T(8,128)(2,1)S(1)} %bitcast.89), channel_id=1, source_target_pairs={{0,1},{1,0},{2,3},{3,2},{4,5},{5,4},{6,7},{7,6},{8,9},{9,8},{10,11... | collective-permute-start | bytes 786440 | tf_op jit(solution)/shard_map/ppermute | solution.py:338
  46.7 7.5 %collective-permute-start.10 = (bf16[128,256]{1,0:T(8,128)(2,1)S(1)}, bf16[128,256]{1,0:T(8,128)(2,1)S(1)}, u32[]{:S(2)}, u32[]{:S(2)}) collective-permute-start(bf16[128,256]{1,0:T(8,128)(2,1)S(1)} %get-tuple-element.78), channel_id=1, source_target_pairs={{0,24},{8,16},{16,8},{24,0},{1,25},{9,17},{17,9},{25,1},{2,26},{10... | collective-permute-start | bytes 196616 | tf_op jit(solution)/shard_map/ppermute | solution.py:338
  46.8 7.4 %collective-permute-start.8 = (bf16[128,256]{1,0:T(8,128)(2,1)S(1)}, bf16[128,256]{1,0:T(8,128)(2,1)S(1)}, u32[]{:S(2)}, u32[]{:S(2)}) collective-permute-start(bf16[128,256]{1,0:T(8,128)(2,1)S(1)} %get-tuple-element.77), channel_id=1, source_target_pairs={{0,8},{8,0},{16,24},{24,16},{1,9},{9,1},{17,25},{25,17},{2,10},{10... | collective-permute-start | bytes 196616 | tf_op jit(solution)/shard_map/ppermute | solution.py:338
  49.3 4.9 %collective-permute-start.9 = (bf16[128,256]{1,0:T(8,128)(2,1)S(1)}, bf16[128,256]{1,0:T(8,128)(2,1)S(1)}, u32[]{:S(2)}, u32[]{:S(2)}) collective-permute-start(bf16[128,256]{1,0:T(8,128)(2,1)S(1)} %get-tuple-element.79), channel_id=1, source_target_pairs={{0,16},{8,24},{16,0},{24,8},{1,17},{9,25},{17,1},{25,9},{2,18},{10... | collective-permute-start | bytes 196616 | tf_op jit(solution)/shard_map/ppermute | solution.py:338
  50.3 7.4 %collective-permute-start.11 = (bf16[2,128,256]{2,1,0:T(8,128)(2,1)S(1)}, bf16[2,128,256]{2,1,0:T(8,128)(2,1)S(1)}, u32[]{:S(2)}, u32[]{:S(2)}) collective-permute-start(bf16[2,128,256]{2,1,0:T(8,128)(2,1)S(1)} %dynamic-slice_bitcast_fusion.1), channel_id=1, source_target_pairs={{0,2},{2,0},{4,6},{6,4},{1,3},{3,1},{5,7},{7,5},{8,10},{10,8},{12,... | collective-permute-start | bytes 393224 | tf_op jit(solution)/shard_map/ppermute | solution.py:338
  57.7 4.5 %collective-permute-start.12 = (bf16[128,256]{1,0:T(8,128)(2,1)S(1)}, bf16[128,256]{1,0:T(8,128)(2,1)S(1)}, u32[]{:S(2)}, u32[]{:S(2)}) collective-permute-start(bf16[128,256]{1,0:T(8,128)(2,1)S(1)} %fusion.6), channel_id=1, source_target_pairs={{0,2},{2,0},{4,6},{6,4},{1,3},{3,1},{5,7},{7,5},{8,10},{10,8},{12,... | collective-permute-start | bytes 196616 | tf_op jit(solution)/shard_map/ppermute | solution.py:338
  59.5 7.0 %collective-permute-start.14 = (bf16[128,256]{1,0:T(8,128)(2,1)S(1)}, bf16[128,256]{1,0:T(8,128)(2,1)S(1)}, u32[]{:S(2)}, u32[]{:S(2)}) collective-permute-start(bf16[128,256]{1,0:T(8,128)(2,1)S(1)} %dynamic-slice_bitcast_fusion.2), channel_id=1, source_target_pairs={{0,4},{2,6},{4,0},{6,2},{1,5},{3,7},{5,1},{7,3},{8,12},{10,14},{12... | collective-permute-start | bytes 196616 | tf_op jit(solution)/shard_map/ppermute | solution.py:338
  62.2 5.2 %collective-permute-start.13 = (bf16[128,256]{1,0:T(8,128)(2,1)S(1)}, bf16[128,256]{1,0:T(8,128)(2,1)S(1)}, u32[]{:S(2)}, u32[]{:S(2)}) collective-permute-start(bf16[128,256]{1,0:T(8,128)(2,1)S(1)} %add_convert_fusion.1), channel_id=1, source_target_pairs={{0,4},{2,6},{4,0},{6,2},{1,5},{3,7},{5,1},{7,3},{8,12},{10,14},{12... | collective-permute-start | bytes 196616 | tf_op jit(solution)/shard_map/ppermute | solution.py:338
  67.5 4.8 %collective-permute-start.15 = (bf16[128,256]{1,0:T(8,128)(2,1)S(1)}, bf16[128,256]{1,0:T(8,128)(2,1)S(1)}, u32[]{:S(2)}, u32[]{:S(2)}) collective-permute-start(bf16[128,256]{1,0:T(8,128)(2,1)S(1)} %add_convert_fusion), channel_id=1, source_target_pairs={{0,8},{8,0},{16,24},{24,16},{1,9},{9,1},{17,25},{25,17},{2,10},{10... | collective-permute-start | bytes 196616 | tf_op jit(solution)/shard_map/ppermute | solution.py:338
  68.2 4.9 %collective-permute-start.16 = (bf16[128,256]{1,0:T(8,128)(2,1)S(1)}, bf16[128,256]{1,0:T(8,128)(2,1)S(1)}, u32[]{:S(2)}, u32[]{:S(2)}) collective-permute-start(bf16[128,256]{1,0:T(8,128)(2,1)S(1)} %add_convert_fusion), channel_id=1, source_target_pairs={{0,16},{8,24},{16,0},{24,8},{1,17},{9,25},{17,1},{25,9},{2,18},{10... | collective-permute-start | bytes 196616 | tf_op jit(solution)/shard_map/ppermute | solution.py:338
  69.7 5.2 %collective-permute-start.17 = (bf16[128,256]{1,0:T(8,128)(2,1)S(1)}, bf16[128,256]{1,0:T(8,128)(2,1)S(1)}, u32[]{:S(2)}, u32[]{:S(2)}) collective-permute-start(bf16[128,256]{1,0:T(8,128)(2,1)S(1)} %add_convert_fusion), channel_id=1, source_target_pairs={{0,24},{8,16},{16,8},{24,0},{1,25},{9,17},{17,9},{25,1},{2,26},{10... | collective-permute-start | bytes 196616 | tf_op jit(solution)/shard_map/ppermute | solution.py:338
  74.9 1.6 %collective-permute-start.18 = (bf16[4,128,256]{2,1,0:T(8,128)(2,1)S(1)}, bf16[4,128,256]{2,1,0:T(8,128)(2,1)S(1)}, u32[]{:S(2)}, u32[]{:S(2)}) collective-permute-start(bf16[4,128,256]{2,1,0:T(8,128)(2,1)S(1)} %bitcast_dynamic-update-slice_fusion.6), channel_id=1, source_target_pairs={{0,1},{1,0},{2,3},{3,2},{4,5},{5,4},{6,7},{7,6},{8,9},{9,8},{10,11... | collective-permute-start | bytes 786440 | tf_op jit(solution)/shard_map/ppermute | solution.py:338

commit v2 on v1

--- a/solution.py
+++ b/solution.py
@@ -40,7 +40,7 @@
     return jnp.broadcast_to(reduced, like.shape)
 
 
-STRIP = 32
+STRIP = 64
 STEP = 256
 
 
@@ -543,9 +543,7 @@
     weights, sources = lax.optimization_barrier((weights, sources))
     weights = scatter_direct(weights.reshape((scans,) + weights.shape[2:]), "scan")
     sources = halve(sources, *source_steps[0])
-    weights, sources, attended, grad_query = lax.optimization_barrier(
-        (weights, sources, attended, grad_query)
-    )
+    weights, attended, grad_query = lax.optimization_barrier((weights, attended, grad_query))
     matched, grad_ref = vmem_call(
         rows_kernel,
         "row_outputs",

time: 77.3 us -> 75.1 us (0.972)
  starting transfers between devices: 27 us -> 20.9 us
  waiting for transfers between devices: 25.2 us -> 29.3 us
    ppermute x19, starting transfers between devices: 27 us -> 20.9 us  [swap(): return lax.ppermute(x, axis, pairs)]
    ppermute x19, waiting for transfers between devices: 25.2 us -> 29.3 us  [swap(): return lax.ppermute(x, axis, pairs)]
  transfers between devices with their start and end apart: 19 -> 19, of which waited for: 16 -> 18; matrix products, arithmetic and copies ran while one was open for 5% -> 5% of each run, Pallas kernels for 3% -> 3%
where the time goes in v2:
time: 75.1 us; the launch traced here: 75.6 us
  waiting for transfers between devices  29.3 us (39%)
  starting transfers between devices  20.9 us (28%)
  Pallas kernels  19.1 us (25%)
  other arithmetic  2.98 us (4%)
  local copies, waits for them, and re-layouts  2.28 us (3%)
  between operations  0.98 us (1%)
    ppermute x19, waiting for transfers between devices, swap(): return lax.ppermute(x, axis, pairs)  29.3 us
    ppermute x19, starting transfers between devices, swap(): return lax.ppermute(x, axis, pairs)  20.9 us
    pallas_call x6, Pallas kernels, vmem_call(): pl.pallas_call(kernel, name=name, out_shape=out_shape, in_specs=specs, ou...  19.1 us
  transfers between devices with their start and end apart: 19, of which 18 were waited for; matrix products, arithmetic and copies ran while one was open for 5% of the time, Pallas kernels for 3%

profile of v2, /device:TPU:0, one launch (start us, length us, event | category | flops | bytes accessed | tf_op | source)
XLA Modules:
  0.0 75.6 jit_solution(3725453177593374012)
XLA Ops:
  0.7 4.1 %collective-permute-start = (bf16[128,256]{1,0:T(8,128)(2,1)}, bf16[128,256]{1,0:T(8,128)(2,1)S(1)}, u32[]{:S(2)}, u32[]{:S(2)}) collective-permute-start(bf16[128,256]{1,0:T(8,128)(2,1)} %bitcast.93), channel_id=1, source_target_pairs={{0,4},{2,6},{4,0},{6,2},{1,5},{3,7},{5,1},{7,3},{8,12},{10,14},{12... | collective-permute-start | bytes 196616 | tf_op jit(solution)/shard_map/ppermute | solution.py:338
  6.3 2.3 %collective-permute-done = bf16[128,256]{1,0:T(8,128)(2,1)S(1)} collective-permute-done((bf16[128,256]{1,0:T(8,128)(2,1)}, bf16[128,256]{1,0:T(8,128)(2,1)S(1)}, u32[]{:S(2)}, u32[]{:S(2)}) %collective-permute-start) | collective-permute-done | bytes 65568 | tf_op jit(solution)/shard_map/ppermute | solution.py:338
  9.4 1.2 %pad_maximum_fusion.near_ref.packed_ref = bf16[1536,256]{1,0:T(8,128)(2,1)S(1)} fusion(bf16[256,256]{1,0:T(8,128)(2,1)} %param.14, bf16[256,256]{1,0:T(8,128)(2,1)} %param.11, bf16[512,256]{1,0:T(8,128)(2,1)} %bitcast.90, bf16[512,256]{1,0:T(8,128)(2,1)} %bitcast.91), kind=kLoop, calls=%fused_computation | loop fusion | flops 3145728 | bytes 1572864 | tf_op jit(solution)/shard_map/concatenate | solution.py:428
  10.7 3.0 %collective-permute-done.1 = bf16[2,128,256]{2,1,0:T(8,128)(2,1)S(1)} collective-permute-done((bf16[2,128,256]{2,1,0:T(8,128)(2,1)S(1)}, bf16[2,128,256]{2,1,0:T(8,128)(2,1)S(1)}, u32[]{:S(2)}, u32[]{:S(2)}) %collective-permute-start.1) | collective-permute-done | bytes 131104 | tf_op jit(solution)/shard_map/ppermute | solution.py:338
  14.2 1.1 %collective-permute-done.2 = bf16[2,2,128,256]{3,2,1,0:T(8,128)(2,1)S(1)} collective-permute-done((bf16[2,2,128,256]{3,2,1,0:T(8,128)(2,1)S(1)}, bf16[2,2,128,256]{3,2,1,0:T(8,128)(2,1)S(1)}, u32[]{:S(2)}, u32[]{:S(2)}) %collective-permute-start.2) | collective-permute-done | bytes 262176 | tf_op jit(solution)/shard_map/ppermute | solution.py:338
  15.3 7.9 %match_stats.1 = (f32[4,512,128]{2,1,0:T(8,128)S(1)}, f32[4,512,128]{2,1,0:T(8,128)S(1)}, f32[3,4,1024]{2,1,0:T(4,128)S(1)}, f32[16,512,256]{2,1,0:T(8,128)S(1)}, bf16[16,512,256]{2,1,0:T(8,128)(2,1)S(1)}) custom-call(s32[4,8]{1,0:T(4,128)S(1)} %select_bitcast_fusion.inter_ref, bf16[4,512,256]{2,1,0:T(8,128)(2,1)S(1)} %get-tuple-element.39.left_ref, ...), custom_call_target="tpu_custom_call" | custom-call | flops 4026531840 | bytes 8388608 | tf_op jit(solution)/shard_map/match_stats/pallas_call | solution.py:399
  23.3 4.3 %collective-permute-done.3 = f32[3,4,1024]{2,1,0:T(4,128)S(1)} collective-permute-done((f32[3,4,1024]{2,1,0:T(4,128)S(1)}, f32[3,4,1024]{2,1,0:T(4,128)S(1)}, u32[]{:S(2)}, u32[]{:S(2)}) %collective-permute-start.3) | collective-permute-done | bytes 49184 | tf_op jit(solution)/shard_map/ppermute | solution.py:338
  27.6 1.4 %collective-permute-start.4 = (f32[3,4,1024]{2,1,0:T(4,128)S(1)}, f32[3,4,1024]{2,1,0:T(4,128)S(1)}, u32[]{:S(2)}, u32[]{:S(2)}) collective-permute-start(f32[3,4,1024]{2,1,0:T(4,128)S(1)} %pad_maximum_fusion.1), channel_id=1, source_target_pairs={{0,4},{2,6},{4,0},{6,2},{1,5},{3,7},{5,1},{7,3},{8,12},{10,14},{12... | collective-permute-start | bytes 147464 | tf_op jit(solution)/shard_map/ppermute | solution.py:338
  29.0 4.1 %collective-permute-done.4 = f32[3,4,1024]{2,1,0:T(4,128)S(1)} collective-permute-done((f32[3,4,1024]{2,1,0:T(4,128)S(1)}, f32[3,4,1024]{2,1,0:T(4,128)S(1)}, u32[]{:S(2)}, u32[]{:S(2)}) %collective-permute-start.4) | collective-permute-done | bytes 49184 | tf_op jit(solution)/shard_map/ppermute | solution.py:338
  34.4 8.7 %match_grads.1 = (bf16[512,256]{1,0:T(8,128)(2,1)S(1)}, bf16[512,256]{1,0:T(8,128)(2,1)S(1)}, bf16[256,1024]{1,0:T(8,128)(2,1)S(1)}, bf16[256,1024]{1,0:T(8,128)(2,1)S(1)}, bf16[4,256,256]{2,1,0:T(8,128)(2,1)S(1)}) custom-call(s32[4,8]{1,0:T(4,128)S(1)} %select_bitcast_fusion.inter_ref, f32[16,512,256]{2,1,0:T(8,128)S(1)} %get-tuple-element.44.score_ref, ...), custom_call_target="tpu_custom_call" | custom-call | flops 6710886400 | bytes 8388608 | tf_op jit(solution)/shard_map/match_grads/pallas_call | solution.py:399
  43.1 1.6 %collective-permute-start.6 = (bf16[2,2,128,256]{3,2,1,0:T(8,128)(2,1)S(1)}, bf16[2,2,128,256]{3,2,1,0:T(8,128)(2,1)S(1)}, u32[]{:S(2)}, u32[]{:S(2)}) collective-permute-start(bf16[2,2,128,256]{3,2,1,0:T(8,128)(2,1)S(1)} %dynamic-slice_bitcast_fusion), channel_id=1, source_target_pairs={{0,1},{1,0},{2,3},{3,2},{4,5},{5,4},{6,7},{7,6},{8,9},{9,8},{10,11... | collective-permute-start | bytes 786440 | tf_op jit(solution)/shard_map/ppermute | solution.py:338
  45.9 1.0 %collective-permute-done.7 = bf16[2,2,128,256]{3,2,0,1:T(8,128)(2,1)S(1)} collective-permute-done((bf16[2,2,128,256]{3,2,0,1:T(8,128)(2,1)S(1)}, bf16[2,2,128,256]{3,2,0,1:T(8,128)(2,1)S(1)}, u32[]{:S(2)}, u32[]{:S(2)}) %collective-permute-start.7) | collective-permute-done | bytes 262176 | tf_op jit(solution)/shard_map/ppermute | solution.py:338
  47.0 2.3 %collective-permute-start.10 = (bf16[128,256]{1,0:T(8,128)(2,1)S(1)}, bf16[128,256]{1,0:T(8,128)(2,1)S(1)}, u32[]{:S(2)}, u32[]{:S(2)}) collective-permute-start(bf16[128,256]{1,0:T(8,128)(2,1)S(1)} %get-tuple-element.76), channel_id=1, source_target_pairs={{0,24},{8,16},{16,8},{24,0},{1,25},{9,17},{17,9},{25,1},{2,26},{10... | collective-permute-start | bytes 196616 | tf_op jit(solution)/shard_map/ppermute | solution.py:338
  49.3 1.2 %collective-permute-start.9 = (bf16[128,256]{1,0:T(8,128)(2,1)S(1)}, bf16[128,256]{1,0:T(8,128)(2,1)S(1)}, u32[]{:S(2)}, u32[]{:S(2)}) collective-permute-start(bf16[128,256]{1,0:T(8,128)(2,1)S(1)} %get-tuple-element.77), channel_id=1, source_target_pairs={{0,16},{8,24},{16,0},{24,8},{1,17},{9,25},{17,1},{25,9},{2,18},{10... | collective-permute-start | bytes 196616 | tf_op jit(solution)/shard_map/ppermute | solution.py:338
  50.6 2.3 %collective-permute-done.10 = bf16[128,256]{1,0:T(8,128)(2,1)S(1)} collective-permute-done((bf16[128,256]{1,0:T(8,128)(2,1)S(1)}, bf16[128,256]{1,0:T(8,128)(2,1)S(1)}, u32[]{:S(2)}, u32[]{:S(2)}) %collective-permute-start.10) | collective-permute-done | bytes 65568 | tf_op jit(solution)/shard_map/ppermute | solution.py:338
  54.0 1.6 %collective-permute-done.13 = bf16[2,128,256]{2,1,0:T(8,128)(2,1)S(1)} collective-permute-done((bf16[2,128,256]{2,1,0:T(8,128)(2,1)S(1)}, bf16[2,128,256]{2,1,0:T(8,128)(2,1)S(1)}, u32[]{:S(2)}, u32[]{:S(2)}) %collective-permute-start.13) | collective-permute-done | bytes 131104 | tf_op jit(solution)/shard_map/ppermute | solution.py:338
  55.7 4.0 %collective-permute-start.14 = (bf16[128,256]{1,0:T(8,128)(2,1)S(1)}, bf16[128,256]{1,0:T(8,128)(2,1)S(1)}, u32[]{:S(2)}, u32[]{:S(2)}) collective-permute-start(bf16[128,256]{1,0:T(8,128)(2,1)S(1)} %dynamic-slice_bitcast_fusion.2), channel_id=1, source_target_pairs={{0,4},{2,6},{4,0},{6,2},{1,5},{3,7},{5,1},{7,3},{8,12},{10,14},{12... | collective-permute-start | bytes 196616 | tf_op jit(solution)/shard_map/ppermute | solution.py:338
  59.7 1.6 %collective-permute-start.12 = (bf16[128,256]{1,0:T(8,128)(2,1)S(1)}, bf16[128,256]{1,0:T(8,128)(2,1)S(1)}, u32[]{:S(2)}, u32[]{:S(2)}) collective-permute-start(bf16[128,256]{1,0:T(8,128)(2,1)S(1)} %add_convert_fusion.1), channel_id=1, source_target_pairs={{0,4},{2,6},{4,0},{6,2},{1,5},{3,7},{5,1},{7,3},{8,12},{10,14},{12... | collective-permute-start | bytes 196616 | tf_op jit(solution)/shard_map/ppermute | solution.py:338
  62.5 2.4 %collective-permute-done.12 = bf16[128,256]{1,0:T(8,128)(2,1)S(1)} collective-permute-done((bf16[128,256]{1,0:T(8,128)(2,1)S(1)}, bf16[128,256]{1,0:T(8,128)(2,1)S(1)}, u32[]{:S(2)}, u32[]{:S(2)}) %collective-permute-start.12) | collective-permute-done | bytes 65568 | tf_op jit(solution)/shard_map/ppermute | solution.py:338
  64.9 2.0 %collective-permute-start.15 = (bf16[128,256]{1,0:T(8,128)(2,1)S(1)}, bf16[128,256]{1,0:T(8,128)(2,1)S(1)}, u32[]{:S(2)}, u32[]{:S(2)}) collective-permute-start(bf16[128,256]{1,0:T(8,128)(2,1)S(1)} %add_convert_fusion), channel_id=1, source_target_pairs={{0,8},{8,0},{16,24},{24,16},{1,9},{9,1},{17,25},{25,17},{2,10},{10... | collective-permute-start | bytes 196616 | tf_op jit(solution)/shard_map/ppermute | solution.py:338
  69.3 1.8 %collective-permute-done.16 = bf16[128,256]{1,0:T(8,128)(2,1)S(1)} collective-permute-done((bf16[128,256]{1,0:T(8,128)(2,1)S(1)}, bf16[128,256]{1,0:T(8,128)(2,1)S(1)}, u32[]{:S(2)}, u32[]{:S(2)}) %collective-permute-start.16) | collective-permute-done | bytes 65568 | tf_op jit(solution)/shard_map/ppermute | solution.py:338
  71.2 1.7 %collective-permute-done.17 = bf16[128,256]{1,0:T(8,128)(2,1)S(1)} collective-permute-done((bf16[128,256]{1,0:T(8,128)(2,1)S(1)}, bf16[128,256]{1,0:T(8,128)(2,1)S(1)}, u32[]{:S(2)}, u32[]{:S(2)}) %collective-permute-start.17) | collective-permute-done | bytes 65568 | tf_op jit(solution)/shard_map/ppermute | solution.py:338
  73.0 1.1 %row_outputs.1 = (bf16[512,256]{1,0:T(8,128)(2,1)}, bf16[512,256]{1,0:T(8,128)(2,1)}) custom-call(bf16[1536,256]{1,0:T(8,128)(2,1)S(1)} %pad_maximum_fusion.near_ref.packed_ref, bf16[512,256]{1,0:T(8,128)(2,1)S(1)} %get-tuple-element.59.attended_ref, bf16[512,256]{1,0:T(8,128)(2,1)S(1)} %get-tuple-element.60.gquery_ref), custom_call_target="tpu_custom_call" | custom-call | flops 268435456 | bytes 2097152 | tf_op jit(solution)/shard_map/row_outputs/pallas_call | solution.py:399
  74.6 1.0 %slice_bitcast_fusion = (f32[256,256]{1,0:T(8,128)}, f32[256,256]{1,0:T(8,128)}, f32[256,256]{1,0:T(8,128)}, f32[256,256]{1,0:T(8,128)}) fusion(f32[4,256,256]{2,1,0:T(8,128)S(1)} %convert.6), kind=kLoop, calls=%fused_computation.5 | loop fusion | bytes 2097152 | tf_op jit(solution)/shard_map/squeeze | solution.py:572
  (65 shorter events, 11.2 us)
Async XLA Ops:
  0.6 10.0 %copy-start = (bf16[256,256]{1,0:T(8,128)(2,1)S(1)}, bf16[256,256]{1,0:T(8,128)(2,1)}, u32[]{:S(2)}) copy-start(bf16[256,256]{1,0:T(8,128)(2,1)} %param.12) | copy-start | bytes 393220
  0.6 10.0 %copy-start.1 = (bf16[256,256]{1,0:T(8,128)(2,1)S(1)}, bf16[256,256]{1,0:T(8,128)(2,1)}, u32[]{:S(2)}) copy-start(bf16[256,256]{1,0:T(8,128)(2,1)} %param.13) | copy-start | bytes 393220
  0.7 8.0 %collective-permute-start = (bf16[128,256]{1,0:T(8,128)(2,1)}, bf16[128,256]{1,0:T(8,128)(2,1)S(1)}, u32[]{:S(2)}, u32[]{:S(2)}) collective-permute-start(bf16[128,256]{1,0:T(8,128)(2,1)} %bitcast.93), channel_id=1, source_target_pairs={{0,4},{2,6},{4,0},{6,2},{1,5},{3,7},{5,1},{7,3},{8,12},{10,14},{12... | collective-permute-start | bytes 196616 | tf_op jit(solution)/shard_map/ppermute | solution.py:338
  8.6 5.0 %collective-permute-start.1 = (bf16[2,128,256]{2,1,0:T(8,128)(2,1)S(1)}, bf16[2,128,256]{2,1,0:T(8,128)(2,1)S(1)}, u32[]{:S(2)}, u32[]{:S(2)}) collective-permute-start(bf16[2,128,256]{2,1,0:T(8,128)(2,1)S(1)} %bitcast_dynamic-update-slice_fusion.10), channel_id=1, source_target_pairs={{0,2},{2,0},{4,6},{6,4},{1,3},{3,1},{5,7},{7,5},{8,10},{10,8},{12,... | collective-permute-start | bytes 393224 | tf_op jit(solution)/shard_map/ppermute | solution.py:338
  13.7 1.6 %collective-permute-start.2 = (bf16[2,2,128,256]{3,2,1,0:T(8,128)(2,1)S(1)}, bf16[2,2,128,256]{3,2,1,0:T(8,128)(2,1)S(1)}, u32[]{:S(2)}, u32[]{:S(2)}) collective-permute-start(bf16[2,2,128,256]{3,2,1,0:T(8,128)(2,1)S(1)} %bitcast_dynamic-update-slice_fusion.5), channel_id=1, source_target_pairs={{0,1},{1,0},{2,3},{3,2},{4,5},{5,4},{6,7},{7,6},{8,9},{9,8},{10,11... | collective-permute-start | bytes 786440 | tf_op jit(solution)/shard_map/ppermute | solution.py:338
  23.2 4.4 %collective-permute-start.3 = (f32[3,4,1024]{2,1,0:T(4,128)S(1)}, f32[3,4,1024]{2,1,0:T(4,128)S(1)}, u32[]{:S(2)}, u32[]{:S(2)}) collective-permute-start(f32[3,4,1024]{2,1,0:T(4,128)S(1)} %get-tuple-element.52.own_ref), channel_id=1, source_target_pairs={{0,2},{2,0},{4,6},{6,4},{1,3},{3,1},{5,7},{7,5},{8,10},{10,8},{12,... | collective-permute-start | bytes 147464 | tf_op jit(solution)/shard_map/ppermute | solution.py:338
  27.6 5.4 %collective-permute-start.4 = (f32[3,4,1024]{2,1,0:T(4,128)S(1)}, f32[3,4,1024]{2,1,0:T(4,128)S(1)}, u32[]{:S(2)}, u32[]{:S(2)}) collective-permute-start(f32[3,4,1024]{2,1,0:T(4,128)S(1)} %pad_maximum_fusion.1), channel_id=1, source_target_pairs={{0,4},{2,6},{4,0},{6,2},{1,5},{3,7},{5,1},{7,3},{8,12},{10,14},{12... | collective-permute-start | bytes 147464 | tf_op jit(solution)/shard_map/ppermute | solution.py:338
  33.1 1.3 %collective-permute-start.5 = (f32[3,4,1024]{2,1,0:T(4,128)S(1)}, f32[3,4,1024]{2,1,0:T(4,128)S(1)}, u32[]{:S(2)}, u32[]{:S(2)}) collective-permute-start(f32[3,4,1024]{2,1,0:T(4,128)S(1)} %pad_maximum_fusion.2.near_ref), channel_id=1, source_target_pairs={{0,1},{1,0},{2,3},{3,2},{4,5},{5,4},{6,7},{7,6},{8,9},{9,8},{10,11... | collective-permute-start | bytes 147464 | tf_op jit(solution)/shard_map/ppermute | solution.py:338
  43.1 2.7 %collective-permute-start.6 = (bf16[2,2,128,256]{3,2,1,0:T(8,128)(2,1)S(1)}, bf16[2,2,128,256]{3,2,1,0:T(8,128)(2,1)S(1)}, u32[]{:S(2)}, u32[]{:S(2)}) collective-permute-start(bf16[2,2,128,256]{3,2,1,0:T(8,128)(2,1)S(1)} %dynamic-slice_bitcast_fusion), channel_id=1, source_target_pairs={{0,1},{1,0},{2,3},{3,2},{4,5},{5,4},{6,7},{7,6},{8,9},{9,8},{10,11... | collective-permute-start | bytes 786440 | tf_op jit(solution)/shard_map/ppermute | solution.py:338
  45.3 1.6 %collective-permute-start.7 = (bf16[2,2,128,256]{3,2,0,1:T(8,128)(2,1)S(1)}, bf16[2,2,128,256]{3,2,0,1:T(8,128)(2,1)S(1)}, u32[]{:S(2)}, u32[]{:S(2)}) collective-permute-start(bf16[2,2,128,256]{3,2,0,1:T(8,128)(2,1)S(1)} %bitcast.89), channel_id=1, source_target_pairs={{0,1},{1,0},{2,3},{3,2},{4,5},{5,4},{6,7},{7,6},{8,9},{9,8},{10,11... | collective-permute-start | bytes 786440 | tf_op jit(solution)/shard_map/ppermute | solution.py:338
  47.0 5.9 %collective-permute-start.10 = (bf16[128,256]{1,0:T(8,128)(2,1)S(1)}, bf16[128,256]{1,0:T(8,128)(2,1)S(1)}, u32[]{:S(2)}, u32[]{:S(2)}) collective-permute-start(bf16[128,256]{1,0:T(8,128)(2,1)S(1)} %get-tuple-element.76), channel_id=1, source_target_pairs={{0,24},{8,16},{16,8},{24,0},{1,25},{9,17},{17,9},{25,1},{2,26},{10... | collective-permute-start | bytes 196616 | tf_op jit(solution)/shard_map/ppermute | solution.py:338
  49.3 4.3 %collective-permute-start.8 = (bf16[128,256]{1,0:T(8,128)(2,1)S(1)}, bf16[128,256]{1,0:T(8,128)(2,1)S(1)}, u32[]{:S(2)}, u32[]{:S(2)}) collective-permute-start(bf16[128,256]{1,0:T(8,128)(2,1)S(1)} %get-tuple-element.75), channel_id=1, source_target_pairs={{0,8},{8,0},{16,24},{24,16},{1,9},{9,1},{17,25},{25,17},{2,10},{10... | collective-permute-start | bytes 196616 | tf_op jit(solution)/shard_map/ppermute | solution.py:338
  49.3 4.5 %collective-permute-start.9 = (bf16[128,256]{1,0:T(8,128)(2,1)S(1)}, bf16[128,256]{1,0:T(8,128)(2,1)S(1)}, u32[]{:S(2)}, u32[]{:S(2)}) collective-permute-start(bf16[128,256]{1,0:T(8,128)(2,1)S(1)} %get-tuple-element.77), channel_id=1, source_target_pairs={{0,16},{8,24},{16,0},{24,8},{1,17},{9,25},{17,1},{25,9},{2,18},{10... | collective-permute-start | bytes 196616 | tf_op jit(solution)/shard_map/ppermute | solution.py:338
  50.6 5.0 %collective-permute-start.13 = (bf16[2,128,256]{2,1,0:T(8,128)(2,1)S(1)}, bf16[2,128,256]{2,1,0:T(8,128)(2,1)S(1)}, u32[]{:S(2)}, u32[]{:S(2)}) collective-permute-start(bf16[2,128,256]{2,1,0:T(8,128)(2,1)S(1)} %dynamic-slice_bitcast_fusion.1), channel_id=1, source_target_pairs={{0,2},{2,0},{4,6},{6,4},{1,3},{3,1},{5,7},{7,5},{8,10},{10,8},{12,... | collective-permute-start | bytes 393224 | tf_op jit(solution)/shard_map/ppermute | solution.py:338
  53.9 5.8 %collective-permute-start.11 = (bf16[128,256]{1,0:T(8,128)(2,1)S(1)}, bf16[128,256]{1,0:T(8,128)(2,1)S(1)}, u32[]{:S(2)}, u32[]{:S(2)}) collective-permute-start(bf16[128,256]{1,0:T(8,128)(2,1)S(1)} %fusion.6), channel_id=1, source_target_pairs={{0,2},{2,0},{4,6},{6,4},{1,3},{3,1},{5,7},{7,5},{8,10},{10,8},{12,... | collective-permute-start | bytes 196616 | tf_op jit(solution)/shard_map/ppermute | solution.py:338
  55.7 6.2 %collective-permute-start.14 = (bf16[128,256]{1,0:T(8,128)(2,1)S(1)}, bf16[128,256]{1,0:T(8,128)(2,1)S(1)}, u32[]{:S(2)}, u32[]{:S(2)}) collective-permute-start(bf16[128,256]{1,0:T(8,128)(2,1)S(1)} %dynamic-slice_bitcast_fusion.2), channel_id=1, source_target_pairs={{0,4},{2,6},{4,0},{6,2},{1,5},{3,7},{5,1},{7,3},{8,12},{10,14},{12... | collective-permute-start | bytes 196616 | tf_op jit(solution)/shard_map/ppermute | solution.py:338
  59.7 5.2 %collective-permute-start.12 = (bf16[128,256]{1,0:T(8,128)(2,1)S(1)}, bf16[128,256]{1,0:T(8,128)(2,1)S(1)}, u32[]{:S(2)}, u32[]{:S(2)}) collective-permute-start(bf16[128,256]{1,0:T(8,128)(2,1)S(1)} %add_convert_fusion.1), channel_id=1, source_target_pairs={{0,4},{2,6},{4,0},{6,2},{1,5},{3,7},{5,1},{7,3},{8,12},{10,14},{12... | collective-permute-start | bytes 196616 | tf_op jit(solution)/shard_map/ppermute | solution.py:338
  64.9 4.4 %collective-permute-start.15 = (bf16[128,256]{1,0:T(8,128)(2,1)S(1)}, bf16[128,256]{1,0:T(8,128)(2,1)S(1)}, u32[]{:S(2)}, u32[]{:S(2)}) collective-permute-start(bf16[128,256]{1,0:T(8,128)(2,1)S(1)} %add_convert_fusion), channel_id=1, source_target_pairs={{0,8},{8,0},{16,24},{24,16},{1,9},{9,1},{17,25},{25,17},{2,10},{10... | collective-permute-start | bytes 196616 | tf_op jit(solution)/shard_map/ppermute | solution.py:338
  66.9 4.3 %collective-permute-start.16 = (bf16[128,256]{1,0:T(8,128)(2,1)S(1)}, bf16[128,256]{1,0:T(8,128)(2,1)S(1)}, u32[]{:S(2)}, u32[]{:S(2)}) collective-permute-start(bf16[128,256]{1,0:T(8,128)(2,1)S(1)} %add_convert_fusion), channel_id=1, source_target_pairs={{0,16},{8,24},{16,0},{24,8},{1,17},{9,25},{17,1},{25,9},{2,18},{10... | collective-permute-start | bytes 196616 | tf_op jit(solution)/shard_map/ppermute | solution.py:338
  67.7 5.2 %collective-permute-start.17 = (bf16[128,256]{1,0:T(8,128)(2,1)S(1)}, bf16[128,256]{1,0:T(8,128)(2,1)S(1)}, u32[]{:S(2)}, u32[]{:S(2)}) collective-permute-start(bf16[128,256]{1,0:T(8,128)(2,1)S(1)} %add_convert_fusion), channel_id=1, source_target_pairs={{0,24},{8,16},{16,8},{24,0},{1,25},{9,17},{17,9},{25,1},{2,26},{10... | collective-permute-start | bytes 196616 | tf_op jit(solution)/shard_map/ppermute | solution.py:338
  72.9 1.6 %collective-permute-start.18 = (bf16[4,128,256]{2,1,0:T(8,128)(2,1)S(1)}, bf16[4,128,256]{2,1,0:T(8,128)(2,1)S(1)}, u32[]{:S(2)}, u32[]{:S(2)}) collective-permute-start(bf16[4,128,256]{2,1,0:T(8,128)(2,1)S(1)} %bitcast_dynamic-update-slice_fusion.6), channel_id=1, source_target_pairs={{0,1},{1,0},{2,3},{3,2},{4,5},{5,4},{6,7},{7,6},{8,9},{9,8},{10,11... | collective-permute-start | bytes 786440 | tf_op jit(solution)/shard_map/ppermute | solution.py:338
